TPU v7x, 32 devices: a whole 2x2x4 slice. The times are simulated.
32 devices in a mesh: groups: 1, orient: 8 (over z, core), cls: 4 (over y, x).
Axes of the slice: x: 2, y: 2, z: 4, core: 2. Of those that a mesh axis runs over, the one named last changes fastest.
Arguments:
- particles: bfloat16 [384, 33024], P(('groups', 'orient', 'cls')), may hold values from -300 to 300
- projections: bfloat16 [8, 8, 33024], P('cls', 'orient')
- ctf: bfloat16 [8, 16512], replicated, may hold values from -1 to 1
- defocus_group: int32 [384], P(('groups', 'orient', 'cls')), may hold values from 0 to 7
- offsets: int32 [384, 2], P(('groups', 'orient', 'cls')), may hold values from -8 to 8
- routes: int32 [384, 4], P(('groups', 'orient', 'cls')), may hold values from 0 to 7, all different within a row; in each aligned block of 12 rows (0 to 11, 12 to 23, ...) at most 6 rows name the same one
Outputs:
- log_evidence: float32 [384], P(('groups', 'orient', 'cls'))
- data_sum: bfloat16 [8, 8, 33024], P(('groups', 'cls'), 'orient')
Inputs may be any that keep to these rules, and one draw needn't show every extreme that they name: `routes`: the 4 blocks of a particle differ; among the particles of one device no block is listed more than 6 times, and some block is listed exactly 6 times.
All inputs are finite; a program needn't handle non-finite values.
Results may differ from a plain program's by a relative error of at most 0.01.
The roundings to bfloat16 on the way count: a program that leaves them out, or rounds other values in their place, can miss the bound.
Values may be sent and summed in bfloat16 or wider, within the bound.
A program may use at most 64 MiB of HBM per device.

v0:
```python
import math

import jax
import jax.numpy as jnp
import numpy as np
from jax import lax
from jax.sharding import PartitionSpec as P

KX = 86
KY = 192
BOX = 256


two_pi = 2.0 * math.pi
highest = lax.Precision.HIGHEST
local_across = np.array([0, 1, -1, 0, 0], dtype=np.int32)
local_down = np.array([0, 0, 0, 1, -1], dtype=np.int32)


def frequencies():
    column = jnp.arange(KX * KY, dtype=jnp.int32)
    return (column // KY, column % KY - KY // 2)


def rotation(shift_across, shift_down, freq_across, freq_down):
    turns = jnp.mod(freq_across * shift_across + freq_down * shift_down, BOX)
    angle = turns.astype(jnp.float32) * (two_pi / BOX)
    return (jnp.cos(angle), jnp.sin(angle))


def combine_stats(peaks, masses):
    top_value = jnp.max(peaks, axis=-1, keepdims=True)
    return top_value[..., 0] + jnp.log(jnp.sum(masses * jnp.exp(peaks - top_value), axis=-1))


def align_images(images, ctf_rows, shifts, freq_across, freq_down, pixel_count):
    real_part = images[:, :pixel_count].astype(jnp.float32)
    imag_part = images[:, pixel_count:].astype(jnp.float32)
    cos_base, sin_base = rotation(
        shifts[:, 0:1], shifts[:, 1:2], freq_across[None, :], freq_down[None, :]
    )
    first = (real_part * cos_base + imag_part * sin_base) * ctf_rows
    second = (imag_part * cos_base - real_part * sin_base) * ctf_rows
    return jnp.concatenate([first, second], axis=1).astype(jnp.bfloat16)


def spread_phase(table, ndim_rest):
    return table.reshape((table.shape[0],) + (1,) * ndim_rest + (table.shape[1],))


def turn_refs(ref_block, cos_shift, sin_shift, pixel_count):
    real_ref = ref_block[..., :pixel_count].astype(jnp.float32)
    imag_ref = ref_block[..., pixel_count:].astype(jnp.float32)
    cos_wide = spread_phase(cos_shift, real_ref.ndim - 1)
    sin_wide = spread_phase(sin_shift, real_ref.ndim - 1)
    first = real_ref[None] * cos_wide - imag_ref[None] * sin_wide
    second = real_ref[None] * sin_wide + imag_ref[None] * cos_wide
    turned = jnp.concatenate([first, second], axis=-1).astype(jnp.bfloat16)
    return (turned, real_ref * real_ref + imag_ref * imag_ref)


def back_rotate(summed, cos_shift, sin_shift, pixel_count):
    cos_wide = spread_phase(cos_shift, summed.ndim - 2)
    sin_wide = spread_phase(sin_shift, summed.ndim - 2)
    real_sum = summed[..., :pixel_count]
    imag_sum = summed[..., pixel_count:]
    first = jnp.sum(real_sum * cos_wide + imag_sum * sin_wide, axis=0)
    second = jnp.sum(imag_sum * cos_wide - real_sum * sin_wide, axis=0)
    return jnp.concatenate([first, second], axis=-1)


def slot_places(route_rows, orient_size):
    targets = route_rows.reshape(-1)
    onehot = (targets[:, None] == jnp.arange(orient_size, dtype=jnp.int32)[None, :]).astype(
        jnp.int32
    )
    before = jnp.cumsum(onehot, axis=0) - onehot
    return (targets, jnp.sum(before * onehot, axis=1))


def per_device(particles, projections, ctf, defocus_group, offsets, routes):
    pixel_count = KX * KY
    own_count = particles.shape[0]
    route_count = routes.shape[1]
    class_local = projections.shape[0]
    directions = projections.shape[1]
    group_count = ctf.shape[0]
    orient_size = lax.axis_size("orient")
    capacity = max(2, (own_count * route_count + orient_size - 1) // orient_size)
    total_slots = orient_size * capacity
    freq_across, freq_down = frequencies()
    ctf_table = ctf.astype(jnp.float32)
    group_onehot = (
        defocus_group[:, None] == jnp.arange(group_count, dtype=jnp.int32)[None, :]
    ).astype(jnp.float32)
    ctf_rows = jnp.dot(group_onehot, ctf_table, precision=highest)
    aligned = align_images(particles, ctf_rows, offsets, freq_across, freq_down, pixel_count)
    targets, orders = slot_places(routes, orient_size)
    slot_ids = targets * capacity + orders
    matches = (slot_ids[None, :] == jnp.arange(total_slots, dtype=jnp.int32)[:, None]).astype(
        jnp.int32
    )
    picked = jnp.sum(matches.reshape(total_slots, own_count, route_count), axis=2)
    send_images = jnp.dot(picked.astype(jnp.bfloat16), aligned, preferred_element_type=jnp.float32)
    send_images = send_images.astype(jnp.bfloat16).reshape(orient_size, capacity, 2 * pixel_count)
    send_codes = jnp.sum(picked * (defocus_group + 1)[None, :], axis=1).reshape(
        orient_size, capacity
    )
    tiles, codes = (
        lax.all_to_all(send_images, "orient", split_axis=0, concat_axis=0, tiled=True),
        lax.all_to_all(send_codes, "orient", split_axis=0, concat_axis=0, tiled=True),
    )
    rows_in = tiles.reshape(total_slots, 2 * pixel_count)
    codes_in = codes.reshape(total_slots)
    slot_groups = (
        codes_in[:, None] - 1 == jnp.arange(group_count, dtype=jnp.int32)[None, :]
    ).astype(jnp.float32)
    occupied = codes_in > 0
    cos_shift, sin_shift = rotation(
        jnp.asarray(local_across, dtype=jnp.int32)[:, None],
        jnp.asarray(local_down, dtype=jnp.int32)[:, None],
        freq_across[None, :],
        freq_down[None, :],
    )
    shift_total = cos_shift.shape[0]
    ctf_square = ctf_table * ctf_table
    ref_piece = lax.all_gather(projections, "cls", axis=0, tiled=True)
    piece_rows = ref_piece.shape[0]
    group_size = 2
    grouped = ref_piece.reshape(piece_rows // group_size, group_size, directions, 2 * pixel_count)

    def one_group(ref_block):
        turned, magnitude = turn_refs(ref_block, cos_shift, sin_shift, pixel_count)
        products = lax.dot_general(
            rows_in,
            turned.reshape(-1, 2 * pixel_count),
            (((1,), (1,)), ((), ())),
            preferred_element_type=jnp.float32,
        )
        energy = lax.dot_general(
            ctf_square,
            magnitude.reshape(group_size * directions, pixel_count),
            (((1,), (1,)), ((), ())),
            precision=highest,
        )
        slot_energy = jnp.dot(slot_groups, energy, precision=highest).reshape(
            total_slots, 1, group_size, directions
        )
        return (
            products.reshape(total_slots, shift_total, group_size, directions) - 0.5 * slot_energy
        )

    stacked = lax.map(one_group, grouped)
    scores = jnp.transpose(stacked, (1, 2, 0, 3, 4)).reshape(
        total_slots, shift_total, piece_rows, directions
    )
    slot_peak = jnp.max(scores, axis=(1, 2, 3))
    slot_mass = jnp.sum(jnp.exp(scores - slot_peak[:, None, None, None]), axis=(1, 2, 3))
    back_peak, back_mass = (
        lax.all_to_all(
            slot_peak.reshape(orient_size, capacity),
            "orient",
            split_axis=0,
            concat_axis=0,
            tiled=True,
        ),
        lax.all_to_all(
            slot_mass.reshape(orient_size, capacity),
            "orient",
            split_axis=0,
            concat_axis=0,
            tiled=True,
        ),
    )
    match_table = matches.astype(jnp.float32)
    entry_peak = jnp.dot(back_peak.reshape(-1), match_table, precision=highest).reshape(
        own_count, route_count
    )
    entry_mass = jnp.dot(back_mass.reshape(-1), match_table, precision=highest).reshape(
        own_count, route_count
    )
    log_evidence = combine_stats(entry_peak, entry_mass)
    slot_value = jnp.dot(picked.astype(jnp.float32), log_evidence, precision=highest).reshape(
        orient_size, capacity
    )
    evidence_in = lax.all_to_all(
        slot_value, "orient", split_axis=0, concat_axis=0, tiled=True
    ).reshape(total_slots)
    live = occupied[:, None, None, None]
    exponent = jnp.where(live, scores - evidence_in[:, None, None, None], 0.0)
    weights = jnp.where(live, jnp.exp(exponent), 0.0).astype(jnp.bfloat16)
    class_group_size = 2

    def one_group(group_index):
        weight_part = lax.dynamic_slice_in_dim(
            weights, group_index * class_group_size, class_group_size, 2
        )
        summed = lax.dot_general(
            weight_part.reshape(total_slots, -1),
            rows_in,
            (((0,), (0,)), ((), ())),
            preferred_element_type=jnp.float32,
        )
        summed = summed.reshape(shift_total, class_group_size, directions, 2 * pixel_count)
        return back_rotate(summed, cos_shift, sin_shift, pixel_count)

    results = lax.map(
        one_group,
        jnp.arange(class_local * lax.axis_size("cls") // class_group_size, dtype=jnp.int32),
    )
    data_sum = lax.psum_scatter(
        results.reshape(class_local * lax.axis_size("cls"), directions, 2 * pixel_count).astype(
            jnp.bfloat16
        ),
        "cls",
        scatter_dimension=0,
        tiled=True,
    )
    return (log_evidence, data_sum)


def solution(mesh):
    placed = (
        P(("groups", "orient", "cls"), None),
        P("cls", "orient", None),
        P(),
        P(("groups", "orient", "cls")),
        P(("groups", "orient", "cls"), None),
        P(("groups", "orient", "cls"), None),
    )
    return jax.shard_map(
        per_device,
        mesh=mesh,
        in_specs=placed,
        out_specs=(P(("groups", "orient", "cls")), P(("groups", "cls"), "orient", None)),
        check_vma=False,
    )
```

profile of v0, /device:TPU:0, one launch (start us, length us, event | category | flops | bytes accessed | tf_op | source)
XLA Modules:
  0.0 305.0 jit_solution(8616529737925251293)
XLA Ops:
  10.0 6.3 %all-to-all-start.1 = ((s32[8,1,6]{2,1,0:T(1,128)}), s32[8,1,6]{2,1,0:T(1,128)S(1)}, u32[]{:S(2)}, u32[]{:S(2)}) async-start(s32[8,1,6]{2,1,0:T(1,128)} %bitcast.3), calls=%async_computation.1 | async-start | bytes 8192 | tf_op jit(solution)/shard_map/all_to_all | solution.py:111
  17.8 6.1 %fusion.38 = (bf16[12,16512]{1,0:T(8,128)(2,1)S(1)}, bf16[12,16512]{1,0:T(8,128)(2,1)S(1)}) fusion(s32[12]{0:T(128)S(1)} %get-tuple-element.313, s32[16512]{0:T(1024)} %get-tuple-element.493, s32[12]{0:T(128)S(1)} %get-tuple-element.312, s32[16512]{0:T(1024)} %get-tuple-element.491, bf16[12,33024]{1,0:T(8,128)(2,1)} %param.12, bf16[8,16512]{1,0:T(8,128)(2,1)} %param.14, ...), kind=kOutput, calls=%fused_computation.63 | convolution fusion | flops 8718432 | bytes 1981584 | tf_op jit(solution)/shard_map/dot_general | solution.py:96
  24.9 2.6 reshape.281
  27.5 5.2 %all-to-all-start = ((bf16[8,6,33024]{2,1,0:T(8,128)(2,1)}), bf16[8,6,33024]{2,1,0:T(8,128)(2,1)}, u32[]{:S(2)}, u32[]{:S(2)}) async-start(bf16[8,6,33024]{2,1,0:T(8,128)(2,1)} %reshape.281), calls=%async_computation | async-start | bytes 8454144 | tf_op jit(solution)/shard_map/all_to_all | solution.py:110
  32.9 15.3 %all_gather.3 = bf16[8,1,33024]{2,1,0:T(2,128)(2,1)S(1)} all-gather(bf16[2,1,33024]{2,1,0:T(2,128)(2,1)S(1)} %copy.39), channel_id=1, replica_groups=mesh['groups'=1,'orient'=8,'cls'=4] {'cls'}, dimensions={0}, use_global_device_ids=true | all-gather | bytes 660480 | tf_op jit(solution)/shard_map/all_gather | solution.py:127
  48.3 3.2 %reduce.6 = bf16[8,33024]{1,0:T(8,128)(2,1)S(1)} reduce(bf16[8,1,33024]{2,1,0:T(2,128)(2,1)S(1)} %all_gather.3, bf16[]{:T(256)} %constant.106), dimensions={1}, to_apply=%all_gather.3.reduce_sub_computation | reduce | bytes 1056770 | tf_op jit(solution)/shard_map/all_gather | solution.py:127
  51.5 1.0 reshape.280
  53.5 74.1 %all-to-all-done = bf16[8,6,33024]{2,1,0:T(8,128)(2,1)} async-done(((bf16[8,6,33024]{2,1,0:T(8,128)(2,1)}), bf16[8,6,33024]{2,1,0:T(8,128)(2,1)}, u32[]{:S(2)}, u32[]{:S(2)}) %all-to-all-start) | async-done | bytes 3170336 | tf_op jit(solution)/shard_map/all_to_all | solution.py:110
  127.5 2.8 reshape.282
  130.4 57.9 %while.24 = (s32[]{:T(128)}, f32[4,48,5,2,1]{1,3,2,4,0:T(2,128)S(1)}, bf16[4,2,1,33024]{3,1,2,0:T(2,128)(2,1)}, bf16[48,33024]{1,0:T(8,128)(2,1)S(1)}, f32[8,165...) while((s32[]{:T(128)}, ...), condition=%wide.region_5.6_spmd.clone.clone, body=%wide.region_4.5_spmd.clone.clone.sunk | while | flops 39077952 | bytes 9925141 | solution.py:153
  130.4 3.1 %fusion.95 = (f32[5,16512]{1,0:T(8,128)S(1)}, f32[5,16512]{1,0:T(8,128)S(1)}) fusion(s32[5]{0:T(128)S(1)} %get-tuple-element.481, s32[16512]{0:T(1024)} %get-tuple-element.482, s32[5]{0:T(128)S(1)} %get-tuple-element.479, s32[16512]{0:T(1024)} %get-tuple-element.480), kind=kLoop, calls=%fused_computation.20.clone.1 | loop fusion | flops 1320960 | bytes 792616 | tf_op jit(solution)/shard_map/cos | solution.py:28
  135.1 1.4 subtract_convert_fusion.2
  136.6 2.3 add.652
  138.8 1.3 sub.142
  140.1 2.1 convolution_bitcast_fusion.5
  142.3 2.3 fusion.96
  144.9 3.1 %fusion.95 = (f32[5,16512]{1,0:T(8,128)S(1)}, f32[5,16512]{1,0:T(8,128)S(1)}) fusion(s32[5]{0:T(128)S(1)} %get-tuple-element.481, s32[16512]{0:T(1024)} %get-tuple-element.482, s32[5]{0:T(128)S(1)} %get-tuple-element.479, s32[16512]{0:T(1024)} %get-tuple-element.480), kind=kLoop, calls=%fused_computation.20.clone.1 | loop fusion | flops 1320960 | bytes 792616 | tf_op jit(solution)/shard_map/cos | solution.py:28
  149.6 1.4 subtract_convert_fusion.2
  151.0 2.3 add.652
  153.3 1.3 sub.142
  154.6 2.1 convolution_bitcast_fusion.5
  156.8 2.3 fusion.96
  159.4 3.1 %fusion.95 = (f32[5,16512]{1,0:T(8,128)S(1)}, f32[5,16512]{1,0:T(8,128)S(1)}) fusion(s32[5]{0:T(128)S(1)} %get-tuple-element.481, s32[16512]{0:T(1024)} %get-tuple-element.482, s32[5]{0:T(128)S(1)} %get-tuple-element.479, s32[16512]{0:T(1024)} %get-tuple-element.480), kind=kLoop, calls=%fused_computation.20.clone.1 | loop fusion | flops 1320960 | bytes 792616 | tf_op jit(solution)/shard_map/cos | solution.py:28
  164.1 1.4 subtract_convert_fusion.2
  165.5 2.3 add.652
  167.8 1.3 sub.142
  169.1 2.1 convolution_bitcast_fusion.5
  171.3 2.3 fusion.96
  173.9 3.1 %fusion.95 = (f32[5,16512]{1,0:T(8,128)S(1)}, f32[5,16512]{1,0:T(8,128)S(1)}) fusion(s32[5]{0:T(128)S(1)} %get-tuple-element.481, s32[16512]{0:T(1024)} %get-tuple-element.482, s32[5]{0:T(128)S(1)} %get-tuple-element.479, s32[16512]{0:T(1024)} %get-tuple-element.480), kind=kLoop, calls=%fused_computation.20.clone.1 | loop fusion | flops 1320960 | bytes 792616 | tf_op jit(solution)/shard_map/cos | solution.py:28
  178.6 1.4 subtract_convert_fusion.2
  180.0 2.3 add.652
  182.3 1.3 sub.142
  183.6 2.1 convolution_bitcast_fusion.5
  185.8 2.3 fusion.96
  189.1 3.3 %all-to-all-start.3 = ((f32[8,1,6]{2,1,0:T(1,128)}), f32[8,1,6]{2,1,0:T(1,128)S(1)}, u32[]{:S(2)}, u32[]{:S(2)}) async-start(f32[8,1,6]{2,1,0:T(1,128)} %bitcast.8), calls=%async_computation.3 | async-start | bytes 8192 | tf_op jit(solution)/shard_map/all_to_all | solution.py:167
  193.2 4.7 %all-to-all-done.3 = f32[8,1,6]{2,1,0:T(1,128)S(1)} async-done(((f32[8,1,6]{2,1,0:T(1,128)}), f32[8,1,6]{2,1,0:T(1,128)S(1)}, u32[]{:S(2)}, u32[]{:S(2)}) %all-to-all-start.3) | async-done | bytes 224 | tf_op jit(solution)/shard_map/all_to_all | solution.py:167
  197.9 3.3 %all-to-all-start.2 = ((f32[8,1,6]{2,1,0:T(1,128)}), f32[8,1,6]{2,1,0:T(1,128)S(1)}, u32[]{:S(2)}, u32[]{:S(2)}) async-start(f32[8,1,6]{2,1,0:T(1,128)} %bitcast.4), calls=%async_computation.2 | async-start | bytes 8192 | tf_op jit(solution)/shard_map/all_to_all | solution.py:160
  202.5 4.1 %all-to-all-done.2 = f32[8,1,6]{2,1,0:T(1,128)S(1)} async-done(((f32[8,1,6]{2,1,0:T(1,128)}), f32[8,1,6]{2,1,0:T(1,128)S(1)}, u32[]{:S(2)}, u32[]{:S(2)}) %all-to-all-start.2) | async-done | bytes 224 | tf_op jit(solution)/shard_map/all_to_all | solution.py:160
  209.0 3.3 %all-to-all-start.4 = ((f32[8,1,6]{2,1,0:T(1,128)}), f32[8,1,6]{2,1,0:T(1,128)S(1)}, u32[]{:S(2)}, u32[]{:S(2)}) async-start(f32[8,1,6]{2,1,0:T(1,128)} %bitcast.13), calls=%async_computation.4 | async-start | bytes 8192 | tf_op jit(solution)/shard_map/all_to_all | solution.py:186
  212.7 5.0 %all-to-all-done.4 = f32[8,1,6]{2,1,0:T(1,128)S(1)} async-done(((f32[8,1,6]{2,1,0:T(1,128)}), f32[8,1,6]{2,1,0:T(1,128)S(1)}, u32[]{:S(2)}, u32[]{:S(2)}) %all-to-all-start.4) | async-done | bytes 224 | tf_op jit(solution)/shard_map/all_to_all | solution.py:186
  218.5 28.0 %while.25 = (s32[]{:T(128)}, bf16[4,2,1,33024]{3,2,1,0:T(2,128)(2,1)}, s32[4]{0:T(128)S(1)}, bf16[48,5,8,1]{0,2,1,3:T(8,128)(2,1)S(1)}, bf16[48,33024]{1,0:T(8,1...) while((s32[]{:T(128)}, ...), condition=%wide.region_13.14_spmd.clone.clone, body=%wide.region_10.13_spmd.clone.clone.sunk | while | flops 34543108 | bytes 8065315 | solution.py:207
  220.3 3.1 %fusion.100 = (f32[5,16512]{1,0:T(8,128)S(1)}, f32[5,16512]{1,0:T(8,128)S(1)}) fusion(s32[5]{0:T(128)S(1)} %get-tuple-element.518, s32[16512]{0:T(1024)} %get-tuple-element.519, s32[5]{0:T(128)S(1)} %get-tuple-element.516, s32[16512]{0:T(1024)} %get-tuple-element.517), kind=kLoop, calls=%fused_computation.47.clone.1 | loop fusion | flops 1320960 | bytes 792616 | tf_op jit(solution)/shard_map/cos | solution.py:28
  227.3 3.1 %fusion.100 = (f32[5,16512]{1,0:T(8,128)S(1)}, f32[5,16512]{1,0:T(8,128)S(1)}) fusion(s32[5]{0:T(128)S(1)} %get-tuple-element.518, s32[16512]{0:T(1024)} %get-tuple-element.519, s32[5]{0:T(128)S(1)} %get-tuple-element.516, s32[16512]{0:T(1024)} %get-tuple-element.517), kind=kLoop, calls=%fused_computation.47.clone.1 | loop fusion | flops 1320960 | bytes 792616 | tf_op jit(solution)/shard_map/cos | solution.py:28
  234.3 3.1 %fusion.100 = (f32[5,16512]{1,0:T(8,128)S(1)}, f32[5,16512]{1,0:T(8,128)S(1)}) fusion(s32[5]{0:T(128)S(1)} %get-tuple-element.518, s32[16512]{0:T(1024)} %get-tuple-element.519, s32[5]{0:T(128)S(1)} %get-tuple-element.516, s32[16512]{0:T(1024)} %get-tuple-element.517), kind=kLoop, calls=%fused_computation.47.clone.1 | loop fusion | flops 1320960 | bytes 792616 | tf_op jit(solution)/shard_map/cos | solution.py:28
  241.3 3.1 %fusion.100 = (f32[5,16512]{1,0:T(8,128)S(1)}, f32[5,16512]{1,0:T(8,128)S(1)}) fusion(s32[5]{0:T(128)S(1)} %get-tuple-element.518, s32[16512]{0:T(1024)} %get-tuple-element.519, s32[5]{0:T(128)S(1)} %get-tuple-element.516, s32[16512]{0:T(1024)} %get-tuple-element.517), kind=kLoop, calls=%fused_computation.47.clone.1 | loop fusion | flops 1320960 | bytes 792616 | tf_op jit(solution)/shard_map/cos | solution.py:28
  246.5 4.8 %convert_reduce_fusion = bf16[4,2,33024]{2,1,0:T(2,128)(2,1)S(1)} fusion(bf16[4,2,1,33024]{3,2,1,0:T(2,128)(2,1)} %get-tuple-element.82), kind=kLoop, calls=%fused_computation.73 | loop fusion | bytes 1056768 | tf_op jit(solution)/shard_map/convert_element_type | solution.py:212
  253.6 42.7 %all-reduce.3.cloned.1.call-done = bf16[8,1,33024]{2,0,1:T(8,128)(2,1)} async-done(((bf16[8,1,33024]{2,0,1:T(8,128)(2,1)}), bf16[8,1,33024]{2,0,1:T(8,128)(2,1)}) %all-reduce.3.cloned.1.call-update) | async-done | bytes 528400
  296.3 1.8 constant_dynamic-slice_fusion.1
  (133 shorter events, 34.9 us)
Async XLA Ops:
  10.0 17.5 %all-to-all-start.1 = ((s32[8,1,6]{2,1,0:T(1,128)}), s32[8,1,6]{2,1,0:T(1,128)S(1)}, u32[]{:S(2)}, u32[]{:S(2)}) async-start(s32[8,1,6]{2,1,0:T(1,128)} %bitcast.3), calls=%async_computation.1 | async-start | bytes 8192 | tf_op jit(solution)/shard_map/all_to_all | solution.py:111
  27.5 5.2 %copy-start.3 = (bf16[2,1,33024]{2,0,1:T(2,128)(2,1)S(1)}, bf16[2,1,33024]{2,0,1:T(2,128)(2,1)}, u32[]{:S(2)}) copy-start(bf16[2,1,33024]{2,0,1:T(2,128)(2,1)} %param.13) | copy-start | bytes 396292
  27.5 100.0 %all-to-all-start = ((bf16[8,6,33024]{2,1,0:T(8,128)(2,1)}), bf16[8,6,33024]{2,1,0:T(8,128)(2,1)}, u32[]{:S(2)}, u32[]{:S(2)}) async-start(bf16[8,6,33024]{2,1,0:T(8,128)(2,1)} %reshape.281), calls=%async_computation | async-start | bytes 8454144 | tf_op jit(solution)/shard_map/all_to_all | solution.py:110
  48.3 4.2 %copy-start.2 = (bf16[8,16512]{1,0:T(8,128)(2,1)S(1)}, bf16[8,16512]{1,0:T(8,128)(2,1)}, u32[]{:S(2)}) copy-start(bf16[8,16512]{1,0:T(8,128)(2,1)} %param.14) | copy-start | bytes 792580
  53.5 76.9 %copy-start.4 = (s32[5]{0:T(128)S(1)}, s32[5]{0:T(128)}, u32[]{:S(2)}) copy-start(s32[5]{0:T(128)} %constant.95.clone) | copy-start | bytes 64
  53.5 76.9 %copy-start.5 = (s32[5]{0:T(128)S(1)}, s32[5]{0:T(128)}, u32[]{:S(2)}) copy-start(s32[5]{0:T(128)} %constant.96.clone) | copy-start | bytes 64
  134.5 0.7 copy-start
  140.1 2.2 copy-start.1
  149.0 0.7 copy-start
  154.6 2.2 copy-start.1
  163.5 0.7 copy-start
  169.1 2.2 copy-start.1
  177.9 0.7 copy-start
  183.6 2.2 copy-start.1
  189.1 8.8 %all-to-all-start.3 = ((f32[8,1,6]{2,1,0:T(1,128)}), f32[8,1,6]{2,1,0:T(1,128)S(1)}, u32[]{:S(2)}, u32[]{:S(2)}) async-start(f32[8,1,6]{2,1,0:T(1,128)} %bitcast.8), calls=%async_computation.3 | async-start | bytes 8192 | tf_op jit(solution)/shard_map/all_to_all | solution.py:167
  197.9 8.7 %all-to-all-start.2 = ((f32[8,1,6]{2,1,0:T(1,128)}), f32[8,1,6]{2,1,0:T(1,128)S(1)}, u32[]{:S(2)}, u32[]{:S(2)}) async-start(f32[8,1,6]{2,1,0:T(1,128)} %bitcast.4), calls=%async_computation.2 | async-start | bytes 8192 | tf_op jit(solution)/shard_map/all_to_all | solution.py:160
  208.1 10.3 %copy-start.6 = (f32[12]{0:T(128)}, f32[12]{0:T(128)S(1)}, u32[]{:S(2)}) copy-start(f32[12]{0:T(128)S(1)} %log_add_fusion) | copy-start | bytes 148
  209.0 8.7 %all-to-all-start.4 = ((f32[8,1,6]{2,1,0:T(1,128)}), f32[8,1,6]{2,1,0:T(1,128)S(1)}, u32[]{:S(2)}, u32[]{:S(2)}) async-start(f32[8,1,6]{2,1,0:T(1,128)} %bitcast.13), calls=%async_computation.4 | async-start | bytes 8192 | tf_op jit(solution)/shard_map/all_to_all | solution.py:186
  212.3 84.0 %all-reduce.3.cloned.1.call-start = ((), (), s32[]{:S(2)}) async-start(), calls=%async_computation.5 | async-start | bytes 1056768
  251.3 1.1 copy-start.7
Sparse Core Ops, SparseCore 0:
  252.5 43.8 all-reduce.2
where the time goes:
time: 307 us; the launch traced here: 305 us
  waiting for transfers between devices  131 us (43%)
  other arithmetic  46.6 us (15%)
  local copies, waits for them, and re-layouts  44 us (14%)
  matrix products  28.7 us (9%)
  starting transfers between devices  21.8 us (7%)
  blocking collectives  15.3 us (5%)
  between operations  14.9 us (5%)
    all_to_all x1, waiting for transfers between devices, per_device(): lax.all_to_all(send_images, 'orient', split_axis=0, concat_axis=0, tiled=...  74.1 us
    unnamed x2, waiting for transfers between devices  42.8 us
    cos x8, other arithmetic, rotation(): return (jnp.cos(angle), jnp.sin(angle))  24.6 us
    all_gather x1, blocking collectives, per_device(): ref_piece = lax.all_gather(projections, 'cls', axis=0, tiled=True)  15.3 us
    dot_general x4, matrix products, one_group(): lax.dot_general(ctf_square, magnitude.reshape(group_size * directions, pi...  9.16 us
    add x4, local copies, waits for them, and re-layouts, turn_refs(): second = real_ref[None] * sin_wide + imag_ref[None] * cos_wide  9.07 us
    dot_general x4, matrix products, one_group(): lax.dot_general(rows_in, turned.reshape(-1, 2 * pixel_count), (((1,), (1,...  8.57 us
    all_to_all x1, starting transfers between devices, per_device(): lax.all_to_all(send_codes, 'orient', split_axis=0, concat_axis=0, tiled=T...  6.33 us
  transfers between devices with their start and end apart: 6, of which 5 were waited for; matrix products, arithmetic and copies ran while one was open for 6% of the time, Pallas kernels for 0%

commit v1 on v0

--- a/solution.py
+++ b/solution.py
@@ -4,6 +4,8 @@
 import jax.numpy as jnp
 import numpy as np
 from jax import lax
+from jax.experimental import pallas as pl
+from jax.experimental.pallas import tpu as pltpu
 from jax.sharding import PartitionSpec as P
 
 KX = 86
@@ -74,11 +76,13 @@
     onehot = (targets[:, None] == jnp.arange(orient_size, dtype=jnp.int32)[None, :]).astype(
         jnp.int32
     )
-    before = jnp.cumsum(onehot, axis=0) - onehot
+    place = jnp.arange(targets.shape[0], dtype=jnp.int32)
+    earlier = (place[None, :] < place[:, None]).astype(jnp.float32)
+    before = jnp.dot(earlier, onehot.astype(jnp.float32), precision=highest).astype(jnp.int32)
     return (targets, jnp.sum(before * onehot, axis=1))
 
 
-def per_device(particles, projections, ctf, defocus_group, offsets, routes):
+def per_device_slots(particles, projections, ctf, defocus_group, offsets, routes):
     pixel_count = KX * KY
     own_count = particles.shape[0]
     route_count = routes.shape[1]
@@ -219,6 +223,290 @@
     return (log_evidence, data_sum)
 
 
+MESH = pl.DeviceIdType.MESH
+ANY = pl.BlockSpec(memory_space=pl.ANY)
+VMEM_BYTES = 48 * 2**20
+f32 = jnp.float32
+bf16 = jnp.bfloat16
+
+
+def place_of(group):
+    o, c = lax.axis_index("orient"), lax.axis_index("cls")
+    return o // group, o % group, c
+
+
+def greet(peers):
+    barrier = pltpu.get_barrier_semaphore()
+    for peer in peers:
+        pl.semaphore_signal(barrier, inc=1, device_id=peer, device_id_type=MESH)
+    pl.semaphore_wait(barrier, len(peers))
+
+
+def remote(src, dst, send, recv, peer):
+    return pltpu.make_async_remote_copy(
+        src_ref=src, dst_ref=dst, send_sem=send, recv_sem=recv,
+        device_id=peer, device_id_type=MESH,
+    )
+
+
+def gather_kernel(group, n_cls, a_ref, p_ref, m_ref, a_out, p_out, m_out,
+                  local, a_send, a_recv, m_send, m_recv, p_send, p_recv, q_send, q_recv, far_sem):
+    hi, m, c = place_of(group)
+    mates = [{"orient": hi * group + (m + s) % group, "cls": c} for s in range(1, group)]
+    owners = [{"orient": hi * group + m, "cls": (c + s) % n_cls} for s in range(1, n_cls)]
+    far = {"orient": (1 - hi) * group + m, "cls": c}
+    greet(mates + owners + [far])
+    far_copy = remote(p_ref, p_out.at[hi, c], far_sem.at[0], far_sem.at[1], far)
+    far_copy.start()
+    own = [
+        pltpu.make_async_copy(a_ref, a_out.at[m], local.at[0]),
+        pltpu.make_async_copy(p_ref, p_out.at[hi, c], local.at[1]),
+        pltpu.make_async_copy(m_ref, m_out.at[m], local.at[2]),
+    ]
+    copies = []
+    for s, peer in enumerate(owners):
+        copies.append(remote(p_ref, p_out.at[hi, c], p_send.at[s], p_recv.at[s], peer))
+    for s, peer in enumerate(mates):
+        copies.append(remote(a_ref, a_out.at[m], a_send.at[s], a_recv.at[s], peer))
+        copies.append(remote(m_ref, m_out.at[m], m_send.at[s], m_recv.at[s], peer))
+    for copy in copies + own:
+        copy.start()
+    far_copy.wait_recv()
+    there = p_out.at[1 - hi, c]
+    passed = [remote(there, there, q_send.at[s], q_recv.at[s], peer) for s, peer in enumerate(owners)]
+    for copy in passed:
+        copy.start()
+    for copy in own:
+        copy.wait()
+    for copy in copies + passed:
+        copy.wait()
+    far_copy.wait_send()
+
+
+def share_kernel(group, s_ref, s_out, local, send, recv):
+    hi, m, c = place_of(group)
+    mates = [{"orient": hi * group + (m + s) % group, "cls": c} for s in range(1, group)]
+    greet(mates)
+    own = pltpu.make_async_copy(s_ref, s_out.at[m], local.at[0])
+    copies = [remote(s_ref, s_out.at[m], send.at[s], recv.at[s], peer) for s, peer in enumerate(mates)]
+    for copy in copies + [own]:
+        copy.start()
+    for copy in copies + [own]:
+        copy.wait()
+
+
+def reduce_kernel(group, n_cls, u_ref, out_ref, land, send_far, land_far,
+                  near_send, near_recv, away_send, away_recv, far_sem):
+    hi, m, c = place_of(group)
+    owners = [{"orient": hi * group + m, "cls": (c + s) % n_cls} for s in range(1, n_cls)]
+    far = {"orient": (1 - hi) * group + m, "cls": c}
+    greet(owners + [far])
+    away, near = [], []
+    for s in range(1, n_cls):
+        to = (c + s) % n_cls
+        away.append(remote(u_ref.at[1 - hi, to], land.at[1, s - 1], away_send.at[s - 1], away_recv.at[s - 1], owners[s - 1]))
+        near.append(remote(u_ref.at[hi, to], land.at[0, s - 1], near_send.at[s - 1], near_recv.at[s - 1], owners[s - 1]))
+    for copy in away + near:
+        copy.start()
+    for copy in away:
+        copy.wait_recv()
+    total = u_ref[1 - hi, c].astype(f32)
+    for s in range(n_cls - 1):
+        total += land[1, s].astype(f32)
+    send_far[...] = total.astype(bf16)
+    far_copy = remote(send_far, land_far, far_sem.at[0], far_sem.at[1], far)
+    far_copy.start()
+    for copy in near:
+        copy.wait_recv()
+    total = u_ref[hi, c].astype(f32)
+    for s in range(n_cls - 1):
+        total += land[0, s].astype(f32)
+    far_copy.wait_recv()
+    out_ref[...] = (total + land_far[...].astype(f32)).astype(bf16)
+    for copy in away + near:
+        copy.wait_send()
+    far_copy.wait_send()
+
+
+def score_kernel(a_ref, p_ref, ctf_ref, tab_ref, full_ref, energy_ref, re, im):
+    halves, n_cls, twice, width = p_ref.shape
+    classes = twice // 2
+    for h in range(halves):
+        for k in range(n_cls):
+            at = (h * n_cls + k) * classes
+            block = p_ref[h, k].astype(f32)
+            re[at : at + classes] = block[:classes]
+            im[at : at + classes] = block[classes:]
+    p, q = re[...], im[...]
+    square = ctf_ref[...].astype(f32)
+    energy = lax.dot_general(
+        square * square, p * p + q * q, (((1,), (1,)), ((), ())),
+        precision=highest, preferred_element_type=f32,
+    )
+    rows = []
+    for turn in range(5):
+        if turn == 0:
+            rows += [p.astype(bf16), q.astype(bf16)]
+            continue
+        axis = (turn - 1) // 2
+        cos, sin = tab_ref[axis : axis + 1], tab_ref[2 + axis : 3 + axis]
+        sin = sin if turn % 2 else -sin
+        rows += [(p * cos - q * sin).astype(bf16), (p * sin + q * cos).astype(bf16)]
+    turned = jnp.concatenate(rows, axis=0)
+    images = jnp.concatenate([a_ref[s] for s in range(a_ref.shape[0])], axis=0)
+    full = lax.dot_general(turned, images, (((1,), (1,)), ((), ())), preferred_element_type=f32)
+
+    @pl.when(pl.program_id(0) == 0)
+    def _():
+        full_ref[...] = jnp.zeros_like(full_ref)
+        energy_ref[...] = jnp.zeros_like(energy_ref)
+
+    full_ref[...] += full
+    energy_ref[...] += energy
+
+
+def sum_kernel(w_ref, a_ref, tab_ref, u_ref):
+    halves, n_cls, twice, width = u_ref.shape
+    classes = twice // 2
+    n = halves * n_cls * classes
+    images = jnp.concatenate([a_ref[s] for s in range(a_ref.shape[0])], axis=0)
+    summed = jnp.dot(w_ref[...], images, preferred_element_type=f32)
+    first, second = summed[:n], summed[n : 2 * n]
+    for turn in range(1, 5):
+        axis = (turn - 1) // 2
+        cos, sin = tab_ref[axis : axis + 1], tab_ref[2 + axis : 3 + axis]
+        sin = sin if turn % 2 else -sin
+        real, imag = summed[2 * n * turn : 2 * n * turn + n], summed[2 * n * turn + n : 2 * n * (turn + 1)]
+        first += real * cos + imag * sin
+        second += imag * cos - real * sin
+    for h in range(halves):
+        for k in range(n_cls):
+            at = (h * n_cls + k) * classes
+            u_ref[h, k, :classes] = first[at : at + classes].astype(bf16)
+            u_ref[h, k, classes:] = second[at : at + classes].astype(bf16)
+
+
+def local_tables():
+    j = np.arange(KX * KY)
+    angles = np.stack([j // KY, j % KY - KY // 2]) * (two_pi / BOX)
+    return np.concatenate([np.cos(angles), np.sin(angles)]).astype(np.float32)
+
+
+def column_block(pixel_count):
+    lanes = pixel_count // 128
+    return 128 * max(d for d in range(1, lanes + 1) if lanes % d == 0 and d <= 48)
+
+
+def per_device_halves(group, particles, projections, ctf, defocus_group, offsets, routes):
+    pix = KX * KY
+    own = particles.shape[0]
+    classes = projections.shape[0]
+    n_groups = ctf.shape[0]
+    n_orient, n_cls = lax.axis_size("orient"), lax.axis_size("cls")
+    hi, m, c = place_of(group)
+    tables = jnp.asarray(local_tables())
+    freq_across, freq_down = frequencies()
+    group_onehot = (defocus_group[:, None] == jnp.arange(n_groups, dtype=jnp.int32)[None, :]).astype(bf16)
+    ctf_rows = jnp.dot(group_onehot, ctf, preferred_element_type=f32)
+    cos_a, sin_a = rotation(offsets[:, 0:1], jnp.zeros_like(offsets[:, 1:2]), jnp.arange(KX)[None, :], 0)
+    cos_b, sin_b = rotation(offsets[:, 1:2], jnp.zeros_like(offsets[:, 1:2]), jnp.arange(KY)[None, :] - KY // 2, 0)
+    turns = jnp.mod(freq_across[None, :] * offsets[:, 0:1] + freq_down[None, :] * offsets[:, 1:2], BOX)
+    angle = turns.astype(f32) * (two_pi / BOX)
+    cos_base, sin_base = jnp.cos(angle), jnp.sin(angle)
+    real_part = particles[:, :pix].astype(f32)
+    imag_part = particles[:, pix:].astype(f32)
+    first = (real_part * cos_base + imag_part * sin_base) * ctf_rows
+    second = (imag_part * cos_base - real_part * sin_base) * ctf_rows
+    aligned = jnp.concatenate([first, second], axis=0).astype(bf16)
+    own_refs = projections.reshape(classes, 2, pix).transpose(1, 0, 2).reshape(2 * classes, pix)
+    listed = jnp.any(routes.T[:, None, :] == jnp.arange(n_orient, dtype=jnp.int32)[None, :, None], axis=0)
+    meta = jnp.concatenate([listed.astype(f32), defocus_group.astype(f32)[None, :]], axis=0)
+    meta = jnp.pad(meta, ((0, -meta.shape[0] % 8), (0, 128 - own)))
+    halves = n_orient // group
+    dma = pltpu.SemaphoreType.DMA
+    images, refs, metas = pl.pallas_call(
+        lambda *r: gather_kernel(group, n_cls, *r),
+        out_shape=(
+            jax.ShapeDtypeStruct((group,) + aligned.shape, bf16),
+            jax.ShapeDtypeStruct((halves, n_cls) + own_refs.shape, bf16),
+            jax.ShapeDtypeStruct((group,) + meta.shape, f32),
+        ),
+        in_specs=[ANY] * 3,
+        out_specs=(ANY,) * 3,
+        scratch_shapes=[dma((3,))] + [dma((group - 1,))] * 4 + [dma((n_cls - 1,))] * 4 + [dma((2,))],
+        compiler_params=pltpu.CompilerParams(collective_id=0, has_side_effects=True),
+    )(aligned, own_refs, meta)
+
+    block = column_block(pix)
+    steps = pix // block
+    kd = halves * n_cls * classes
+    rows = 5 * 2 * kd
+    wide = group * 2 * own
+    image_spec = pl.BlockSpec((group, 2 * own, block), lambda i: (0, 0, i))
+    table_spec = pl.BlockSpec((4, block), lambda i: (0, i))
+    stack_spec = pl.BlockSpec((halves, n_cls, 2 * classes, block), lambda i: (0, 0, 0, i))
+    full, energy = pl.pallas_call(
+        score_kernel,
+        grid=(steps,),
+        out_shape=(jax.ShapeDtypeStruct((rows, wide), f32), jax.ShapeDtypeStruct((n_groups, kd), f32)),
+        in_specs=[image_spec, stack_spec, pl.BlockSpec((n_groups, block), lambda i: (0, i)), table_spec],
+        out_specs=(pl.BlockSpec((rows, wide), lambda i: (0, 0)), pl.BlockSpec((n_groups, kd), lambda i: (0, 0))),
+        scratch_shapes=[pltpu.VMEM((kd, block), f32)] * 2,
+        compiler_params=pltpu.CompilerParams(vmem_limit_bytes=VMEM_BYTES),
+    )(images, refs, ctf, tables)
+
+    full = full.reshape(5, 2, kd, group, 2, own)
+    scores = full[:, 0, :, :, 0] + full[:, 1, :, :, 1]
+    groups_of = metas[:, n_orient, :own]
+    onehot = (groups_of[:, :, None] == jnp.arange(n_groups, dtype=f32)).astype(f32)
+    scores = scores - 0.5 * jnp.einsum("sig,gk->ksi", onehot, energy, precision=highest)[None]
+    mine = jnp.stack([lax.dynamic_index_in_dim(metas, h * group + m, 1, False)[:, :own] for h in range(halves)])
+    live = jnp.repeat(mine > 0, n_cls * classes, axis=0)[None]
+    masked = jnp.where(live, scores, -jnp.inf)
+    peak = jnp.max(masked, axis=(0, 1))
+    safe = jnp.where(jnp.any(mine > 0, axis=0), peak, -3e38)
+    mass = jnp.sum(jnp.where(live, jnp.exp(jnp.where(live, scores - safe, 0.0)), 0.0), axis=(0, 1))
+    stats = jnp.stack([safe, mass]).reshape(2, group * own)
+    stats = jnp.pad(stats, ((0, 6), (0, 128 - group * own)))
+    shared = pl.pallas_call(
+        lambda *r: share_kernel(group, *r),
+        out_shape=jax.ShapeDtypeStruct((group, 8, 128), f32),
+        in_specs=[ANY],
+        out_specs=ANY,
+        scratch_shapes=[dma((1,)), dma((group - 1,)), dma((group - 1,))],
+        compiler_params=pltpu.CompilerParams(collective_id=1, has_side_effects=True),
+    )(stats)
+    peaks, masses = shared[:, 0, : group * own], shared[:, 1, : group * own]
+    top = jnp.max(peaks, axis=0)
+    evidence = (top + jnp.log(jnp.sum(masses * jnp.exp(peaks - top), axis=0))).reshape(group, own)
+    log_evidence = lax.dynamic_index_in_dim(evidence, m, 0, False)
+    weight = jnp.where(live, jnp.exp(jnp.where(live, scores - evidence, 0.0)), 0.0).astype(bf16)
+    zero = jnp.zeros_like(weight)
+    spread = jnp.stack([jnp.stack([weight, zero], axis=3), jnp.stack([zero, weight], axis=3)], axis=1)
+    sums = pl.pallas_call(
+        sum_kernel,
+        grid=(steps,),
+        out_shape=jax.ShapeDtypeStruct(refs.shape, bf16),
+        in_specs=[pl.BlockSpec((rows, wide), lambda i: (0, 0)), image_spec, table_spec],
+        out_specs=stack_spec,
+        compiler_params=pltpu.CompilerParams(vmem_limit_bytes=VMEM_BYTES),
+    )(spread.reshape(rows, wide), images, tables)
+
+    VM = pl.BlockSpec(memory_space=pltpu.VMEM)
+    piece = (2 * classes, pix)
+    out = pl.pallas_call(
+        lambda *r: reduce_kernel(group, n_cls, *r),
+        out_shape=jax.ShapeDtypeStruct(piece, bf16),
+        in_specs=[VM],
+        out_specs=VM,
+        scratch_shapes=[pltpu.VMEM((2, n_cls - 1) + piece, bf16), pltpu.VMEM(piece, bf16), pltpu.VMEM(piece, bf16)]
+        + [dma((n_cls - 1,))] * 4 + [dma((2,))],
+        compiler_params=pltpu.CompilerParams(collective_id=2, has_side_effects=True, vmem_limit_bytes=VMEM_BYTES),
+    )(sums)
+    data_sum = out.reshape(2, classes, pix).transpose(1, 0, 2).reshape(classes, 1, 2 * pix)
+    return (log_evidence, data_sum)
+
+
 def solution(mesh):
     placed = (
         P(("groups", "orient", "cls"), None),
@@ -228,6 +516,17 @@
         P(("groups", "orient", "cls"), None),
         P(("groups", "orient", "cls"), None),
     )
+
+    def per_device(particles, projections, *rest):
+        group = mesh.shape["orient"] // 2
+        held = 2 * particles.size * group
+        fits = mesh.shape["orient"] == 2 * group and group > 1 and mesh.shape["cls"] > 1
+        fits = fits and 4 * held <= VMEM_BYTES and group * particles.shape[0] <= 128
+        fits = fits and projections.shape[1] == 1
+        if fits:
+            return per_device_halves(group, particles, projections, *rest)
+        return per_device_slots(particles, projections, *rest)
+
     return jax.shard_map(
         per_device,
         mesh=mesh,

time: 307 us -> 103 us (0.34)
  waiting for transfers between devices: 131 us -> 0 us
  Pallas kernels: 0 us -> 69.9 us
  other arithmetic: 46.6 us -> 6.67 us
  local copies, waits for them, and re-layouts: 44 us -> 18.5 us
  matrix products: 28.7 us -> 6.26 us
  starting transfers between devices: 21.8 us -> 0 us
  blocking collectives: 15.3 us -> 0 us
  between operations: 14.9 us -> 0.8 us
    all_to_all x5 -> x0, waiting for transfers between devices: 87.9 us -> none  [the longest x1 74.1 us: per_device(): lax.all_to_all(send_images, 'orient', split_axis=0, concat_axis=0, tiled=...]
    pallas_call x0 -> x5, Pallas kernels: none -> 69.9 us  [the longest x1 41.7 us: per_device_halves(): pl.pallas_call(lambda *r: gather_kernel(group, n_cls, *r), out_shape=(jax...]
    unnamed x2 -> x0, waiting for transfers between devices: 42.8 us -> none
    cos x8 -> x0, other arithmetic: 24.6 us -> none  [rotation(): return (jnp.cos(angle), jnp.sin(angle))]
    dot_general x21 -> x2, matrix products: 28.7 us -> 6.26 us  [the longest x1 6.06 us: per_device_halves(): ctf_rows = jnp.dot(group_onehot, ctf, preferred_element_type=f32)]
    all_to_all x5 -> x0, starting transfers between devices: 21.5 us -> none  [the longest x1 6.33 us: per_device(): lax.all_to_all(send_codes, 'orient', split_axis=0, concat_axis=0, tiled=T...]
    all_gather x1 -> x0, blocking collectives: 15.3 us -> none  [per_device(): ref_piece = lax.all_gather(projections, 'cls', axis=0, tiled=True)]
    add x4 -> x2, local copies, waits for them, and re-layouts: 9.07 us -> 0.18 us  [per_device_halves(): top + jnp.log(jnp.sum(masses * jnp.exp(peaks - top), axis=0))]
  transfers between devices with their start and end apart: 6 -> 0, of which waited for: 5 -> 0; matrix products, arithmetic and copies ran while one was open for 6% -> 0% of each run, Pallas kernels for 0% -> 0%
where the time goes in v1:
time: 103 us; the launch traced here: 102 us
  Pallas kernels  69.9 us (68%)
  local copies, waits for them, and re-layouts  18.5 us (18%)
  other arithmetic  6.67 us (6%)
  matrix products  6.26 us (6%)
    pallas_call x1, Pallas kernels, per_device_halves(): pl.pallas_call(lambda *r: gather_kernel(group, n_cls, *r), out_shape=(jax...  41.7 us
    pallas_call x1, Pallas kernels, per_device_halves(): pl.pallas_call(lambda *r: reduce_kernel(group, n_cls, *r), out_shape=jax....  17.1 us
    unnamed x18, local copies, waits for them, and re-layouts  6.81 us
    dot_general x1, matrix products, per_device_halves(): ctf_rows = jnp.dot(group_onehot, ctf, preferred_element_type=f32)  6.06 us
    pallas_call x1, Pallas kernels, per_device_halves(): pl.pallas_call(lambda *r: share_kernel(group, *r), out_shape=jax.ShapeDty...  5.52 us
    reshape x2, local copies, waits for them, and re-layouts, per_device_halves(): spread.reshape(rows, wide)  3.48 us
    pallas_call x1, Pallas kernels, per_device_halves(): pl.pallas_call(score_kernel, grid=(steps,), out_shape=(jax.ShapeDtypeStru...  3.32 us
    pallas_call x1, Pallas kernels, per_device_halves(): pl.pallas_call(sum_kernel, grid=(steps,), out_shape=jax.ShapeDtypeStruct(...  2.27 us

profile of v1, /device:TPU:0, one launch (start us, length us, event | category | flops | bytes accessed | tf_op | source)
XLA Modules:
  0.0 102.1 jit_solution(8861057495746184739)
XLA Ops:
  0.6 0.8 slice_bitcast_fusion.3
  1.4 6.1 %fusion.2 = (bf16[12,16512]{1,0:T(8,128)(2,1)S(1)}, bf16[12,16512]{1,0:T(8,128)(2,1)S(1)}) fusion(s32[12]{0:T(128)S(1)} %get-tuple-element.25, s32[16512]{0:T(1024)S(1)} %get-tuple-element.27, s32[12]{0:T(128)S(1)} %get-tuple-element.24, s32[16512]{0:T(1024)S(1)} %get-tuple-element.26, bf16[12,33024]{1,0:T(8,128)(2,1)} %param.7, ...), kind=kOutput, calls=%fused_computation.10 | convolution fusion | flops 8718432 | bytes 1981584 | tf_op jit(solution)/shard_map/dot_general | solution.py:410
  7.5 0.0 copy-start.5
  7.5 0.0 copy-start.7
  7.5 0.0 copy-start.6
  7.5 1.1 %pad_maximum_fusion.r_0_ = bf16[24,16512]{1,0:T(8,128)(2,1)} fusion(bf16[12,16512]{1,0:T(8,128)(2,1)S(1)} %get-tuple-element.15, bf16[12,16512]{1,0:T(8,128)(2,1)S(1)} %get-tuple-element.14), kind=kLoop, calls=%fused_computation.17 | loop fusion | flops 1585152 | bytes 1585152 | tf_op jit(solution)/shard_map/concatenate | solution.py:420
  8.6 0.0 copy-done.5
  8.6 0.9 reshape.132.r_1_
  9.5 0.0 copy-done.7
  9.5 0.0 copy-done.6
  9.5 0.6 select_maximum_fusion.r_2_
  10.1 41.7 %shard_map.86 = (bf16[4,24,16512]{2,1,0:T(8,128)(2,1)}, bf16[2,4,4,16512]{3,2,1,0:T(4,128)(2,1)}, f32[4,16,128]{2,1,0:T(8,128)}) custom-call(bf16[24,16512]{1,0:T(8,128)(2,1)} %pad_maximum_fusion.r_0_, bf16[4,16512]{1,0:T(4,128)(2,1)} %reshape.132.r_1_, f32[16,128]{1,0:T(8,128)} %select_maximum_fusion.r_2_), custom_call_target="tpu_custom_call" | custom-call | tf_op jit(solution)/shard_map/pallas_call | solution.py:427
  51.8 0.8 constant_dynamic-slice_fusion.2
  52.7 0.7 slice.41
  53.4 0.0 copy-done.2
  53.4 0.0 copy-done.4
  53.4 1.9 %copy-done = bf16[4,24,16512]{2,1,0:T(8,128)(2,1)S(1)} copy-done((bf16[4,24,16512]{2,1,0:T(8,128)(2,1)S(1)}, bf16[4,24,16512]{2,1,0:T(8,128)(2,1)}, u32[]{:S(2)}) %copy-start) | copy-done | bytes 3170328
  55.3 1.2 %copy-done.3 = bf16[2,4,4,16512]{3,2,1,0:T(4,128)(2,1)S(1)} copy-done((bf16[2,4,4,16512]{3,2,1,0:T(4,128)(2,1)S(1)}, bf16[2,4,4,16512]{3,2,1,0:T(4,128)(2,1)}, u32[]{:S(2)}) %copy-start.3) | copy-done | bytes 1056792
  56.5 3.3 %shard_map.87 = (f32[160,96]{1,0:T(8,128)S(1)}, f32[8,16]{1,0:T(8,128)S(1)}) custom-call(bf16[4,24,16512]{2,1,0:T(8,128)(2,1)S(1)} %copy-done, bf16[2,4,4,16512]{3,2,1,0:T(4,128)(2,1)S(1)} %copy-done.3, bf16[8,16512]{1,0:T(8,128)(2,1)S(1)} %copy-done.4, f32[4,16512]{1,0:T(4,128)S(1)} %copy-done.2), custom_call_target="tpu_custom_call" | custom-call | tf_op jit(solution)/shard_map/pallas_call | solution.py:448
  59.8 0.2 convolution_multiply_fusion
  60.0 0.1 copy.97
  60.2 0.1 copy.93
  60.3 0.9 reshape.139
  61.2 1.1 %fusion.31 = (f32[5,1,16,4,1,12]{5,4,3,2,1,0:T(1,128)}, f32[5,1,16,4,1,12]{5,4,3,2,1,0:T(1,128)}) fusion(f32[5,2,16,4,2,12]{5,4,3,2,1,0:T(2,128)S(1)} %reshape.139), kind=kLoop, calls=%fused_computation.73 | loop fusion | bytes 61440 | tf_op jit(solution)/shard_map/slice | solution.py:459
  62.2 1.9 %copy.112 = f32[5,1,16,4,1,12]{2,3,5,4,1,0:T(4,128)} copy(f32[5,1,16,4,1,12]{5,4,3,2,1,0:T(1,128)} %get-tuple-element.17) | data formatting | bytes 30720
  64.1 1.8 %copy.113 = f32[5,1,16,4,1,12]{2,3,5,4,1,0:T(4,128)} copy(f32[5,1,16,4,1,12]{5,4,3,2,1,0:T(1,128)} %get-tuple-element.16) | data formatting | bytes 30720
  65.9 1.1 %select_reduce_fusion.1 = f32[4,12]{0,1:T(8,128)S(1)} fusion(f32[16,4,12]{0,1,2:T(4,128)S(1)} %copy.97, pred[16,4,12]{0,1,2:T(4,128)(4,1)S(1)} %copy.93, f32[5,1,16,4,1,12]{2,3,5,4,1,0:T(4,128)} %copy.112, f32[5,1,16,4,1,12]{2,3,5,4,1,0:T(4,128)} %copy.113), kind=kLoop, calls=%fused_computation.38 | loop fusion | flops 15312 | bytes 34752 | tf_op jit(solution)/shard_map/reduce_max | solution.py:466
  67.0 0.1 copy.98
  67.1 0.1 copy.99
  67.2 1.2 %select_reduce_fusion = f32[4,12]{0,1:T(8,128)S(1)} fusion(f32[4,12]{0,1:T(8,128)S(1)} %copy.99, f32[16,4,12]{0,1,2:T(4,128)S(1)} %copy.97, pred[16,4,12]{0,1,2:T(4,128)(4,1)S(1)} %copy.93, f32[5,1,16,4,1,12]{2,3,5,4,1,0:T(4,128)} %copy.112, f32[5,1,16,4,1,12]{2,3,5,4,1,0:T(4,128)} %copy.113), kind=kLoop, calls=%fused_computation.37 | loop fusion | flops 22992 | bytes 34944 | tf_op jit(solution)/shard_map/reduce_sum | solution.py:468
  68.4 0.1 copy.100
  68.5 0.1 stack.36
  68.5 0.1 select_n.100
  68.6 0.6 select_maximum_fusion.1.r_0_
  69.2 5.5 %shard_map.88 = f32[4,8,128]{2,1,0:T(8,128)} custom-call(f32[8,128]{1,0:T(8,128)} %select_maximum_fusion.1.r_0_), custom_call_target="tpu_custom_call" | custom-call | tf_op jit(solution)/shard_map/pallas_call | solution.py:471
  74.8 0.8 fusion.32
  75.6 0.1 add.96
  75.7 0.5 fusion.29
  76.2 0.1 copy.104
  76.3 1.1 %fusion.19 = bf16[5,16,4,1,12]{1,2,4,0,3:T(4,128)(2,1)S(1)} fusion(f32[4,12]{0,1:T(8,128)S(1)} %copy.104, f32[16,4,12]{0,1,2:T(4,128)S(1)} %copy.97, pred[16,4,12]{0,1,2:T(4,128)(4,1)S(1)} %copy.93, f32[5,1,16,4,1,12]{2,3,5,4,1,0:T(4,128)} %copy.112, f32[5,1,16,4,1,12]{2,3,5,4,1,0:T(4,128)} %copy.113), kind=kLoop, calls=%fused_computation.33 | loop fusion | flops 23040 | bytes 42432 | tf_op jit(solution)/shard_map/convert_element_type | solution.py:483
  77.4 0.1 pad_bitcast_fusion.1
  77.5 0.9 pad_maximum_fusion.1
  78.4 2.2 %copy.108 = bf16[5,2,16,4,2,12]{5,4,3,2,1,0:T(2,128)(2,1)} copy(bf16[5,2,16,4,2,12]{2,3,5,0,4,1:T(4,128)(2,1)} %pad_maximum_fusion.1) | data formatting | bytes 61440 | tf_op jit(solution)/shard_map/reshape | solution.py:493
  80.6 1.2 %reshape.138.w_ref = bf16[160,96]{1,0:T(8,128)(2,1)S(1)} reshape(bf16[5,2,16,4,2,12]{5,4,3,2,1,0:T(2,128)(2,1)} %copy.108) | data formatting | bytes 61440 | tf_op jit(solution)/shard_map/reshape | solution.py:493
  81.8 0.0 copy-done.1
  81.9 2.3 %shard_map.89.r_0_ = bf16[2,4,4,16512]{3,2,1,0:T(4,128)(2,1)S(1)} custom-call(bf16[160,96]{1,0:T(8,128)(2,1)S(1)} %reshape.138.w_ref, bf16[4,24,16512]{2,1,0:T(8,128)(2,1)S(1)} %copy-done.1, f32[4,16512]{1,0:T(4,128)S(1)} %copy-done.2), custom_call_target="tpu_custom_call" | custom-call | tf_op jit(solution)/shard_map/pallas_call | solution.py:486
  84.1 17.1 %shard_map.90 = bf16[4,16512]{1,0:T(4,128)(2,1)S(1)} custom-call(bf16[2,4,4,16512]{3,2,1,0:T(4,128)(2,1)S(1)} %shard_map.89.r_0_), custom_call_target="tpu_custom_call" | custom-call | tf_op jit(solution)/shard_map/pallas_call | solution.py:497
  101.3 0.8 reshape.135
  (18 shorter events, 0.2 us)
Async XLA Ops:
  7.5 1.1 %copy-start.5 = (bf16[2,1,33024]{2,0,1:T(2,128)(2,1)S(1)}, bf16[2,1,33024]{2,0,1:T(2,128)(2,1)}, u32[]{:S(2)}) copy-start(bf16[2,1,33024]{2,0,1:T(2,128)(2,1)} %param.8) | copy-start | bytes 396292
  7.5 2.0 %copy-start.7 = (s32[12]{0:T(128)S(1)}, s32[12]{0:T(128)}, u32[]{:S(2)}) copy-start(s32[12]{0:T(128)} %param.10) | copy-start | bytes 148
  7.5 2.0 %copy-start.6 = (s32[12,4]{0,1:T(4,128)S(1)}, s32[12,4]{0,1:T(4,128)}, u32[]{:S(2)}) copy-start(s32[12,4]{0,1:T(4,128)} %param.12) | copy-start | bytes 580
  8.6 44.8 %copy-start.2 = (f32[4,16512]{1,0:T(4,128)S(1)}, f32[4,16512]{1,0:T(4,128)}, u32[]{:S(2)}) copy-start(f32[4,16512]{1,0:T(4,128)} %constant.87.clone.tab_ref) | copy-start | bytes 792580
  8.6 44.8 %copy-start.4 = (bf16[8,16512]{1,0:T(8,128)(2,1)S(1)}, bf16[8,16512]{1,0:T(8,128)(2,1)}, u32[]{:S(2)}) copy-start(bf16[8,16512]{1,0:T(8,128)(2,1)} %ctf_ref.1) | copy-start | bytes 792580
  53.4 1.9 %copy-start = (bf16[4,24,16512]{2,1,0:T(8,128)(2,1)S(1)}, bf16[4,24,16512]{2,1,0:T(8,128)(2,1)}, u32[]{:S(2)}) copy-start(bf16[4,24,16512]{2,1,0:T(8,128)(2,1)} %get-tuple-element.8.a_ref) | copy-start | bytes 9510916
  55.3 1.2 %copy-start.3 = (bf16[2,4,4,16512]{3,2,1,0:T(4,128)(2,1)S(1)}, bf16[2,4,4,16512]{3,2,1,0:T(4,128)(2,1)}, u32[]{:S(2)}) copy-start(bf16[2,4,4,16512]{3,2,1,0:T(4,128)(2,1)} %get-tuple-element.9.p_ref) | copy-start | bytes 3170308
  62.2 19.6 %copy-start.1 = (bf16[4,24,16512]{2,1,0:T(8,128)(2,1)S(1)}, bf16[4,24,16512]{2,1,0:T(8,128)(2,1)}, u32[]{:S(2)}) copy-start(bf16[4,24,16512]{2,1,0:T(8,128)(2,1)} %get-tuple-element.8.a_ref) | copy-start | bytes 9510916

commit v2 on v0

--- a/solution.py
+++ b/solution.py
@@ -1,9 +1,12 @@
+import functools
 import math
 
 import jax
 import jax.numpy as jnp
 import numpy as np
 from jax import lax
+from jax.experimental import pallas as pl
+from jax.experimental.pallas import tpu as pltpu
 from jax.sharding import PartitionSpec as P
 
 KX = 86
@@ -74,11 +77,13 @@
     onehot = (targets[:, None] == jnp.arange(orient_size, dtype=jnp.int32)[None, :]).astype(
         jnp.int32
     )
-    before = jnp.cumsum(onehot, axis=0) - onehot
+    place = jnp.arange(targets.shape[0], dtype=jnp.int32)
+    earlier = (place[None, :] < place[:, None]).astype(jnp.float32)
+    before = jnp.dot(earlier, onehot.astype(jnp.float32), precision=highest).astype(jnp.int32)
     return (targets, jnp.sum(before * onehot, axis=1))
 
 
-def per_device(particles, projections, ctf, defocus_group, offsets, routes):
+def per_device_slots(particles, projections, ctf, defocus_group, offsets, routes):
     pixel_count = KX * KY
     own_count = particles.shape[0]
     route_count = routes.shape[1]
@@ -219,6 +224,278 @@
     return (log_evidence, data_sum)
 
 
+MESH = pl.DeviceIdType.MESH
+VMEM_BYTES = 48 * 2**20
+f32 = jnp.float32
+bf16 = jnp.bfloat16
+
+
+def place_of(group):
+    o, c = lax.axis_index("orient"), lax.axis_index("cls")
+    return o // group, o % group, c
+
+
+def greet(peers):
+    barrier = pltpu.get_barrier_semaphore()
+    for peer in peers:
+        pl.semaphore_signal(barrier, inc=1, device_id=peer, device_id_type=MESH)
+    pl.semaphore_wait(barrier, len(peers))
+
+
+def remote(src, dst, send, recv, peer):
+    return pltpu.make_async_remote_copy(
+        src_ref=src, dst_ref=dst, send_sem=send, recv_sem=recv,
+        device_id=peer, device_id_type=MESH,
+    )
+
+
+def turn_of(tables, turn, columns):
+    axis = (turn - 1) // 2
+    cos, sin = tables[axis : axis + 1, columns], tables[2 + axis : 3 + axis, columns]
+    return cos, (sin if turn % 2 else -sin)
+
+
+def fused_kernel(group, n_cls, own, pieces,
+                 a_ref, p_ref, m_ref, ctf_ref, tables,
+                 sum_out, evidence_out,
+                 images, refs, metas, re, im, full, stats, sums, land, send_far, land_far,
+                 x_send, x_recv, s_send, s_recv, f_send, f_recv, m_send, m_recv,
+                 p_send, p_recv, q_send, q_recv, far_sem, e_send, e_recv,
+                 near_send, near_recv, away_send, away_recv, back_sem, local):
+    hi, m, c = place_of(group)
+    pix = a_ref.shape[1]
+    width = pix // pieces
+    classes = p_ref.shape[0] // 2
+    n_groups = ctf_ref.shape[0]
+    kd = 2 * n_cls * classes
+    used = 2 * own * group
+    sibling = m + 1 - 2 * (m % 2)
+    at = lambda member: {"orient": hi * group + member, "cls": c}
+    mates = [at((m + s) % group) for s in range(1, group)]
+    hops = group // 2 - 1
+    owners = [{"orient": hi * group + m, "cls": (c + s) % n_cls} for s in range(1, n_cls)]
+    far = {"orient": (1 - hi) * group + m, "cls": c}
+    greet(mates + owners + [far])
+
+    far_copy = remote(p_ref, refs.at[hi, c], far_sem.at[0], far_sem.at[1], far)
+    far_copy.start()
+    kept = [
+        pltpu.make_async_copy(a_ref, images.at[m], local.at[0]),
+        pltpu.make_async_copy(p_ref, refs.at[hi, c], local.at[1]),
+        pltpu.make_async_copy(m_ref, metas.at[m], local.at[2]),
+    ]
+    first = [remote(p_ref, refs.at[hi, c], p_send.at[s], p_recv.at[s], peer) for s, peer in enumerate(owners)]
+    cols = [pl.ds(q * width, width) for q in range(pieces)]
+    crossing, beside, onward = [], [], []
+    for q in range(pieces):
+        for k in range(hops):
+            crossing.append(remote(a_ref.at[:, cols[q]], images.at[m, :, cols[q]], x_send.at[q, k], x_recv.at[q, k],
+                                   at((m + 2 * (k + 1)) % group)))
+            slot = images.at[(m + group - 2 * (k + 1)) % group, :, cols[q]]
+            onward.append(remote(slot, slot, f_send.at[q, k], f_recv.at[q, k], at(sibling)))
+        beside.append(remote(a_ref.at[:, cols[q]], images.at[m, :, cols[q]], s_send.at[q], s_recv.at[q], at(sibling)))
+    told = [remote(m_ref, metas.at[m], m_send.at[s], m_recv.at[s], peer) for s, peer in enumerate(mates)]
+    for copy in crossing + first + beside + told + kept:
+        copy.start()
+    far_copy.wait_recv()
+    there = refs.at[1 - hi, c]
+    passed = [remote(there, there, q_send.at[s], q_recv.at[s], peer) for s, peer in enumerate(owners)]
+    for copy in passed:
+        copy.start()
+    full[...] = jnp.zeros_like(full)
+    for copy in kept:
+        copy.wait()
+    for copy in first + passed:
+        copy.wait_recv()
+
+    def all_images(q):
+        return jnp.concatenate([images[s, :, q * width : (q + 1) * width] for s in range(group)], axis=0)
+
+    def score_piece(q):
+        here = slice(q * width, (q + 1) * width)
+        for h in range(2):
+            for k in range(n_cls):
+                row = (h * n_cls + k) * classes
+                block = refs[h, k, :, here].astype(f32)
+                re[row : row + classes] = block[:classes]
+                im[row : row + classes] = block[classes:]
+        p, q_ = re[...], im[...]
+        square = ctf_ref[:, here].astype(f32)
+        energy = lax.dot_general(p * p + q_ * q_, square * square, (((1,), (1,)), ((), ())),
+                                 precision=highest, preferred_element_type=f32)
+        rows = [p.astype(bf16), q_.astype(bf16)]
+        for turn in range(1, 5):
+            cos, sin = turn_of(tables, turn, here)
+            rows += [(p * cos - q_ * sin).astype(bf16), (p * sin + q_ * cos).astype(bf16)]
+        turned = jnp.concatenate(rows, axis=0)
+        for copy in onward[q * hops : (q + 1) * hops] + [beside[q]]:
+            copy.wait_recv()
+        full[:, :used] += lax.dot_general(turned, all_images(q), (((1,), (1,)), ((), ())), preferred_element_type=f32)
+        return energy
+
+    energy = jnp.zeros((kd, n_groups), f32)
+    for q in range(pieces):
+        for copy, pass_on in zip(crossing[q * hops : (q + 1) * hops], onward[q * hops : (q + 1) * hops]):
+            copy.wait_recv()
+            pass_on.start()
+        if q:
+            energy += score_piece(q - 1)
+    energy += score_piece(pieces - 1)
+    for copy in told:
+        copy.wait_recv()
+
+    lanes = full.shape[1]
+    meta = metas[0]
+    for s in range(1, group):
+        meta += pltpu.roll(metas[s], 2 * own * s, 1)
+    n_orient = 2 * group
+    listed, onehot = meta[:n_orient], meta[n_orient : n_orient + n_groups]
+    level = jnp.dot(energy, onehot, precision=highest, preferred_element_type=f32)
+    row_of = lax.broadcasted_iota(jnp.int32, listed.shape, 0)
+    mine = [jnp.sum(jnp.where(row_of == h * group + m, listed, 0.0), axis=0, keepdims=True) for h in range(2)]
+    live = jnp.concatenate([jnp.broadcast_to(row, (kd // 2, lanes)) for row in mine], axis=0) > 0
+    score = []
+    for turn in range(5):
+        real, imag = full[2 * kd * turn : 2 * kd * turn + kd], full[2 * kd * turn + kd : 2 * kd * (turn + 1)]
+        score.append(real + pltpu.roll(imag, lanes - own, 1) - 0.5 * level)
+    low = -3.0e38
+    peak = functools.reduce(jnp.maximum, score)
+    peak = jnp.max(jnp.where(live, peak, low), axis=0, keepdims=True)
+    mass = sum(jnp.where(live, jnp.exp(jnp.where(live, v - peak, 0.0)), 0.0) for v in score)
+    mass = jnp.sum(mass, axis=0, keepdims=True)
+    half_row = lax.broadcasted_iota(jnp.int32, (8, lanes), 0)
+    stats[m] = jnp.where(half_row == 0, peak, jnp.where(half_row == 1, mass, 0.0))
+    shared = [remote(stats.at[m], stats.at[m], e_send.at[s], e_recv.at[s], peer) for s, peer in enumerate(mates)]
+    for copy in shared:
+        copy.start()
+    for copy in shared:
+        copy.wait_recv()
+    held = [stats[s] for s in range(group)]
+    top = functools.reduce(jnp.maximum, [v[0:1] for v in held])
+    evidence = top + jnp.log(sum(v[1:2] * jnp.exp(v[0:1] - top) for v in held))
+    result = jnp.zeros((8, lanes), f32)
+    wide = jnp.broadcast_to(evidence, (8, lanes))
+    for s in range(group):
+        moved = pltpu.roll(wide, lanes - 2 * own * s, 1) if s else wide
+        result = jnp.where(m == s, moved, result)
+    evidence_out[...] = result
+    weights = []
+    for value in score:
+        weight = jnp.where(live, jnp.exp(jnp.where(live, value - evidence, 0.0)), 0.0)
+        weights += [weight.astype(bf16), pltpu.roll(weight, own, 1).astype(bf16)]
+    weights = jnp.concatenate(weights, axis=0)[:, :used]
+
+    away, near = [], []
+    for s in range(1, n_cls):
+        to = (c + s) % n_cls
+        away.append(remote(sums.at[1 - hi, to], land.at[1, s - 1], away_send.at[s - 1], away_recv.at[s - 1], owners[s - 1]))
+        near.append(remote(sums.at[hi, to], land.at[0, s - 1], near_send.at[s - 1], near_recv.at[s - 1], owners[s - 1]))
+    for q in range(pieces):
+        here = slice(q * width, (q + 1) * width)
+        summed = jnp.dot(weights, all_images(q), preferred_element_type=f32)
+        real_sum, imag_sum = summed[:kd], summed[kd : 2 * kd]
+        for turn in range(1, 5):
+            cos, sin = turn_of(tables, turn, here)
+            real, imag = summed[2 * kd * turn : 2 * kd * turn + kd], summed[2 * kd * turn + kd : 2 * kd * (turn + 1)]
+            real_sum += real * cos + imag * sin
+            imag_sum += imag * cos - real * sin
+        for h in range(2):
+            for k in range(n_cls):
+                row = (h * n_cls + k) * classes
+                sums[h, k, :classes, here] = real_sum[row : row + classes].astype(bf16)
+                sums[h, k, classes:, here] = imag_sum[row : row + classes].astype(bf16)
+    for copy in away + near:
+        copy.start()
+    for copy in away:
+        copy.wait_recv()
+    total = sums[1 - hi, c].astype(f32)
+    for s in range(n_cls - 1):
+        total += land[1, s].astype(f32)
+    send_far[...] = total.astype(bf16)
+    back = remote(send_far, land_far, back_sem.at[0], back_sem.at[1], far)
+    back.start()
+    for copy in near:
+        copy.wait_recv()
+    total = sums[hi, c].astype(f32)
+    for s in range(n_cls - 1):
+        total += land[0, s].astype(f32)
+    back.wait_recv()
+    sum_out[...] = (total + land_far[...].astype(f32)).astype(bf16)
+    for copy in [far_copy, back] + first + passed + crossing + beside + onward + told + shared + away + near:
+        copy.wait_send()
+
+
+def local_tables():
+    j = np.arange(KX * KY)
+    angles = np.stack([j // KY, j % KY - KY // 2]) * (two_pi / BOX)
+    return np.concatenate([np.cos(angles), np.sin(angles)]).astype(np.float32)
+
+
+def column_block(pixel_count):
+    lanes = pixel_count // 128
+    return 128 * max(d for d in range(1, lanes + 1) if lanes % d == 0 and d <= 48)
+
+
+def per_device_halves(group, particles, projections, ctf, defocus_group, offsets, routes):
+    pix = KX * KY
+    own = particles.shape[0]
+    classes = projections.shape[0]
+    n_groups = ctf.shape[0]
+    n_orient, n_cls = lax.axis_size("orient"), lax.axis_size("cls")
+    tables = jnp.asarray(local_tables())
+    freq_across, freq_down = frequencies()
+    group_onehot = (defocus_group[:, None] == jnp.arange(n_groups, dtype=jnp.int32)[None, :]).astype(bf16)
+    ctf_rows = jnp.dot(group_onehot, ctf, preferred_element_type=f32)
+    turns = jnp.mod(freq_across[None, :] * offsets[:, 0:1] + freq_down[None, :] * offsets[:, 1:2], BOX)
+    angle = turns.astype(f32) * (two_pi / BOX)
+    cos_base, sin_base = jnp.cos(angle), jnp.sin(angle)
+    real_part = particles[:, :pix].astype(f32)
+    imag_part = particles[:, pix:].astype(f32)
+    first = (real_part * cos_base + imag_part * sin_base) * ctf_rows
+    second = (imag_part * cos_base - real_part * sin_base) * ctf_rows
+    aligned = jnp.concatenate([first, second], axis=0).astype(bf16)
+    own_refs = projections.reshape(classes, 2, pix).transpose(1, 0, 2).reshape(2 * classes, pix)
+    listed = jnp.any(routes.T[:, None, :] == jnp.arange(n_orient, dtype=jnp.int32)[None, :, None], axis=0)
+    chosen = jnp.arange(n_groups, dtype=jnp.int32)[:, None] == defocus_group[None, :]
+    meta = jnp.concatenate([listed, chosen], axis=0).astype(f32)
+    meta = jnp.pad(meta, ((0, -meta.shape[0] % 8), (0, 128 - own)))
+    block = column_block(pix)
+    pieces = pix // block
+    kd = 2 * n_cls * classes
+    dma = pltpu.SemaphoreType.DMA
+    vmem = pltpu.VMEM
+    spec = pl.BlockSpec(memory_space=pltpu.VMEM)
+    piece = own_refs.shape
+    stack = (2, n_cls) + piece
+    hops = group // 2 - 1
+    out, evidence = pl.pallas_call(
+        lambda *r: fused_kernel(group, n_cls, own, pieces, *r),
+        out_shape=(jax.ShapeDtypeStruct(piece, bf16), jax.ShapeDtypeStruct((8, 128), f32)),
+        in_specs=[spec] * 5,
+        out_specs=(spec, spec),
+        scratch_shapes=[
+            vmem((group,) + aligned.shape, bf16),
+            vmem(stack, bf16),
+            vmem((group,) + meta.shape, f32),
+            vmem((kd, block), f32),
+            vmem((kd, block), f32),
+            vmem((10 * kd, 128), f32),
+            vmem((group, 8, 128), f32),
+            vmem(stack, bf16),
+            vmem((2, n_cls - 1) + piece, bf16),
+            vmem(piece, bf16),
+            vmem(piece, bf16),
+        ]
+        + [dma((pieces, hops))] * 2 + [dma((pieces,))] * 2 + [dma((pieces, hops))] * 2 + [dma((group - 1,))] * 2
+        + [dma((n_cls - 1,))] * 4 + [dma((2,))] + [dma((group - 1,))] * 2
+        + [dma((n_cls - 1,))] * 4 + [dma((2,)), dma((3,))],
+        compiler_params=pltpu.CompilerParams(collective_id=0, has_side_effects=True, vmem_limit_bytes=VMEM_BYTES),
+    )(aligned, own_refs, meta, ctf, tables)
+    log_evidence = evidence[0, :own]
+    data_sum = out.reshape(2, classes, pix).transpose(1, 0, 2).reshape(classes, 1, 2 * pix)
+    return (log_evidence, data_sum)
+
+
 def solution(mesh):
     placed = (
         P(("groups", "orient", "cls"), None),
@@ -228,6 +505,17 @@
         P(("groups", "orient", "cls"), None),
         P(("groups", "orient", "cls"), None),
     )
+
+    def per_device(particles, projections, *rest):
+        group = mesh.shape["orient"] // 2
+        held = 2 * particles.size * group
+        fits = mesh.shape["orient"] == 2 * group and group > 2 and group % 2 == 0 and mesh.shape["cls"] > 1
+        fits = fits and 4 * held <= VMEM_BYTES and 2 * group * particles.shape[0] <= 128
+        fits = fits and projections.shape[1] == 1
+        if fits:
+            return per_device_halves(group, particles, projections, *rest)
+        return per_device_slots(particles, projections, *rest)
+
     return jax.shard_map(
         per_device,
         mesh=mesh,

time: 307 us -> 61.5 us (0.20)
  waiting for transfers between devices: 131 us -> 0 us
  Pallas kernels: 0 us -> 51.3 us
  other arithmetic: 46.6 us -> 0.26 us
  local copies, waits for them, and re-layouts: 44 us -> 3.01 us
  matrix products: 28.7 us -> 6.05 us
  starting transfers between devices: 21.8 us -> 0 us
  blocking collectives: 15.3 us -> 0 us
  between operations: 14.9 us -> 0.76 us
    all_to_all x5 -> x0, waiting for transfers between devices: 87.9 us -> none  [the longest x1 74.1 us: per_device(): lax.all_to_all(send_images, 'orient', split_axis=0, concat_axis=0, tiled=...]
    pallas_call x0 -> x1, Pallas kernels: none -> 51.3 us  [per_device_halves(): pl.pallas_call(lambda *r: fused_kernel(group, n_cls, own, pieces, *r), ou...]
    unnamed x2 -> x0, waiting for transfers between devices: 42.8 us -> none
    cos x8 -> x0, other arithmetic: 24.6 us -> none  [rotation(): return (jnp.cos(angle), jnp.sin(angle))]
    dot_general x21 -> x1, matrix products: 28.7 us -> 6.05 us  [per_device_halves(): ctf_rows = jnp.dot(group_onehot, ctf, preferred_element_type=f32)]
    all_to_all x5 -> x0, starting transfers between devices: 21.5 us -> none  [the longest x1 6.33 us: per_device(): lax.all_to_all(send_codes, 'orient', split_axis=0, concat_axis=0, tiled=T...]
    all_gather x1 -> x0, blocking collectives: 15.3 us -> none  [per_device(): ref_piece = lax.all_gather(projections, 'cls', axis=0, tiled=True)]
    add x4 -> x0, local copies, waits for them, and re-layouts: 9.07 us -> none  [turn_refs(): second = real_ref[None] * sin_wide + imag_ref[None] * cos_wide]
  transfers between devices with their start and end apart: 6 -> 0, of which waited for: 5 -> 0; matrix products, arithmetic and copies ran while one was open for 6% -> 0% of each run, Pallas kernels for 0% -> 0%
where the time goes in v2:
time: 61.5 us; the launch traced here: 61.4 us
  Pallas kernels  51.3 us (83%)
  matrix products  6.05 us (10%)
  local copies, waits for them, and re-layouts  3.01 us (5%)
  between operations  0.76 us (1%)
    pallas_call x1, Pallas kernels, per_device_halves(): pl.pallas_call(lambda *r: fused_kernel(group, n_cls, own, pieces, *r), ou...  51.3 us
    dot_general x1, matrix products, per_device_halves(): ctf_rows = jnp.dot(group_onehot, ctf, preferred_element_type=f32)  6.05 us

profile of v2, /device:TPU:0, one launch (start us, length us, event | category | flops | bytes accessed | tf_op | source)
XLA Modules:
  0.0 61.4 jit_solution(7536120024980141067)
XLA Ops:
  0.7 0.8 %slice_bitcast_fusion.2 = (s32[12]{0:T(128)S(1)}, s32[12]{0:T(128)S(1)}) fusion(s32[12,2]{0,1:T(2,128)} %param.11), kind=kLoop, calls=%fused_computation.41 | loop fusion | bytes 192 | tf_op jit(solution)/shard_map/mul | solution.py:449
  1.4 6.0 %fusion.2 = (bf16[12,16512]{1,0:T(8,128)(2,1)S(1)}, bf16[12,16512]{1,0:T(8,128)(2,1)S(1)}) fusion(s32[12]{0:T(128)S(1)} %get-tuple-element.9, s32[16512]{0:T(1024)S(1)} %get-tuple-element.11, s32[12]{0:T(128)S(1)} %get-tuple-element.8, s32[16512]{0:T(1024)S(1)} %get-tuple-element.10, bf16[12,33024]{1,0:T(8,128)(2,1)} %param.7, bf16[8,16512]{1,0:T(8,128)(2,1)} %r_3_.1, ...), kind=kOutput, calls=%fused_computation.9 | convolution fusion | flops 8718432 | bytes 1981584 | tf_op jit(solution)/shard_map/dot_general | solution.py:448
  7.5 0.0 copy-start.2
  7.5 0.0 copy-start.3
  7.5 0.0 copy-start.4
  7.5 0.0 copy-start
  7.5 0.0 copy-start.1
  7.5 0.2 pad_maximum_fusion.r_0_
  7.7 0.6 %copy-done.2 = bf16[2,1,33024]{2,0,1:T(2,128)(2,1)S(1)} copy-done((bf16[2,1,33024]{2,0,1:T(2,128)(2,1)S(1)}, bf16[2,1,33024]{2,0,1:T(2,128)(2,1)}, u32[]{:S(2)}) %copy-start.2) | copy-done | bytes 132120
  8.4 0.2 reshape.40.r_1_
  8.6 0.0 copy-done.3
  8.6 0.0 copy-done.4
  8.7 0.0 copy-done
  8.7 0.0 copy-done.1
  8.7 51.3 %shard_map.86 = (bf16[4,16512]{1,0:T(4,128)(2,1)S(1)}, f32[8,128]{1,0:T(8,128)S(1)}) custom-call(bf16[24,16512]{1,0:T(8,128)(2,1)S(1)} %pad_maximum_fusion.r_0_, bf16[4,16512]{1,0:T(4,128)(2,1)S(1)} %reshape.40.r_1_, f32[16,128]{1,0:T(8,128)S(1)} %pad_convert_fusion.r_2_, bf16[8,16512]{1,0:T(8,128)(2,1)S(1)} %copy-done, f32[4,16512]{1,0:T(4,128)S(1)} %copy-done.1), custom_call_target="tpu_custom_call" | custom-call | tf_op jit(solution)/shard_map/pallas_call | solution.py:471
  60.0 0.8 %reshape.41 = bf16[2,2,16512]{2,1,0:T(2,128)(2,1)} reshape(bf16[4,16512]{1,0:T(4,128)(2,1)S(1)} %get-tuple-element.5) | data formatting | bytes 264192 | tf_op jit(solution)/shard_map/reshape | solution.py:495
  60.9 0.5 slice_bitcast_fusion
  (5 shorter events, 0.1 us)
Async XLA Ops:
  7.5 0.9 %copy-start.2 = (bf16[2,1,33024]{2,0,1:T(2,128)(2,1)S(1)}, bf16[2,1,33024]{2,0,1:T(2,128)(2,1)}, u32[]{:S(2)}) copy-start(bf16[2,1,33024]{2,0,1:T(2,128)(2,1)} %param.8) | copy-start | bytes 396292
  7.5 1.1 %copy-start.3 = (s32[12,4]{0,1:T(4,128)S(1)}, s32[12,4]{0,1:T(4,128)}, u32[]{:S(2)}) copy-start(s32[12,4]{0,1:T(4,128)} %param.12) | copy-start | bytes 580
  7.5 1.1 %copy-start.4 = (s32[12]{0:T(128)S(1)}, s32[12]{0:T(128)}, u32[]{:S(2)}) copy-start(s32[12]{0:T(128)} %param.10) | copy-start | bytes 148
  7.5 1.2 %copy-start = (bf16[8,16512]{1,0:T(8,128)(2,1)S(1)}, bf16[8,16512]{1,0:T(8,128)(2,1)}, u32[]{:S(2)}) copy-start(bf16[8,16512]{1,0:T(8,128)(2,1)} %r_3_.1) | copy-start | bytes 792580
  7.5 1.2 %copy-start.1 = (f32[4,16512]{1,0:T(4,128)S(1)}, f32[4,16512]{1,0:T(4,128)}, u32[]{:S(2)}) copy-start(f32[4,16512]{1,0:T(4,128)} %constant.46.clone.r_4_) | copy-start | bytes 792580

commit v3 on v2

--- a/solution.py
+++ b/solution.py
@@ -256,14 +256,14 @@
 
 
 def fused_kernel(group, n_cls, own, pieces,
-                 a_ref, p_ref, m_ref, ctf_ref, tables,
+                 x_ref, phase_ref, chosen_ref, p_ref, m_ref, ctf_ref, tables,
                  sum_out, evidence_out,
-                 images, refs, metas, re, im, full, stats, sums, land, send_far, land_far,
+                 ctf_rows, images, refs, metas, re, im, full, stats, sums, land, send_far, land_far,
                  x_send, x_recv, s_send, s_recv, f_send, f_recv, m_send, m_recv,
                  p_send, p_recv, q_send, q_recv, far_sem, e_send, e_recv,
                  near_send, near_recv, away_send, away_recv, back_sem, local):
     hi, m, c = place_of(group)
-    pix = a_ref.shape[1]
+    pix = x_ref.shape[1] // 2
     width = pix // pieces
     classes = p_ref.shape[0] // 2
     n_groups = ctf_ref.shape[0]
@@ -280,23 +280,51 @@
     far_copy = remote(p_ref, refs.at[hi, c], far_sem.at[0], far_sem.at[1], far)
     far_copy.start()
     kept = [
-        pltpu.make_async_copy(a_ref, images.at[m], local.at[0]),
-        pltpu.make_async_copy(p_ref, refs.at[hi, c], local.at[1]),
-        pltpu.make_async_copy(m_ref, metas.at[m], local.at[2]),
+        pltpu.make_async_copy(p_ref, refs.at[hi, c], local.at[0]),
+        pltpu.make_async_copy(m_ref, metas.at[m], local.at[1]),
     ]
     first = [remote(p_ref, refs.at[hi, c], p_send.at[s], p_recv.at[s], peer) for s, peer in enumerate(owners)]
     cols = [pl.ds(q * width, width) for q in range(pieces)]
     crossing, beside, onward = [], [], []
     for q in range(pieces):
         for k in range(hops):
-            crossing.append(remote(a_ref.at[:, cols[q]], images.at[m, :, cols[q]], x_send.at[q, k], x_recv.at[q, k],
+            crossing.append(remote(images.at[m, :, cols[q]], images.at[m, :, cols[q]], x_send.at[q, k], x_recv.at[q, k],
                                    at((m + 2 * (k + 1)) % group)))
             slot = images.at[(m + group - 2 * (k + 1)) % group, :, cols[q]]
             onward.append(remote(slot, slot, f_send.at[q, k], f_recv.at[q, k], at(sibling)))
-        beside.append(remote(a_ref.at[:, cols[q]], images.at[m, :, cols[q]], s_send.at[q], s_recv.at[q], at(sibling)))
+        beside.append(remote(images.at[m, :, cols[q]], images.at[m, :, cols[q]], s_send.at[q], s_recv.at[q], at(sibling)))
     told = [remote(m_ref, metas.at[m], m_send.at[s], m_recv.at[s], peer) for s, peer in enumerate(mates)]
-    for copy in crossing + first + beside + told + kept:
+    for copy in first + told + kept:
         copy.start()
+
+    period = phase_ref.shape[1] - 1
+    step_cos, step_sin = phase_ref[0, period], phase_ref[1, period]
+    blocks = width // 128
+
+    def align_block(phases, q, offset):
+        cos, sin = phases[0]
+        there = pl.ds(pl.multiple_of(q * width + offset, 128), 128)
+        mirror = pl.ds(pl.multiple_of(pix + q * width + offset, 128), 128)
+        real, imag = x_ref[:, there].astype(f32), x_ref[:, mirror].astype(f32)
+        scale = ctf_rows[:, pl.ds(pl.multiple_of(offset, 128), 128)]
+        both = [(real * cos + imag * sin) * scale, (imag * cos - real * sin) * scale]
+        images[m, :, there] = jnp.concatenate(both, axis=0).astype(bf16)
+        ahead = (cos * step_cos - sin * step_sin, sin * step_cos + cos * step_sin)
+        return phases[1:] + [ahead]
+
+    def align_some(i, phases, q):
+        for u in range(period):
+            phases = align_block(phases, q, (i * period + u) * 128)
+        return phases
+
+    phases = [(phase_ref[0, u], phase_ref[1, u]) for u in range(period)]
+    for q in range(pieces):
+        ctf_rows[...] = jnp.dot(chosen_ref[...], ctf_ref[:, q * width : (q + 1) * width], preferred_element_type=f32)
+        phases = lax.fori_loop(0, blocks // period, functools.partial(align_some, q=q), phases)
+        for u in range(blocks % period):
+            phases = align_block(phases, q, (blocks // period * period + u) * 128)
+        for copy in crossing[q * hops : (q + 1) * hops] + [beside[q]]:
+            copy.start()
     far_copy.wait_recv()
     there = refs.at[1 - hi, c]
     passed = [remote(there, there, q_send.at[s], q_recv.at[s], peer) for s, peer in enumerate(owners)]
@@ -443,17 +471,13 @@
     n_groups = ctf.shape[0]
     n_orient, n_cls = lax.axis_size("orient"), lax.axis_size("cls")
     tables = jnp.asarray(local_tables())
-    freq_across, freq_down = frequencies()
     group_onehot = (defocus_group[:, None] == jnp.arange(n_groups, dtype=jnp.int32)[None, :]).astype(bf16)
-    ctf_rows = jnp.dot(group_onehot, ctf, preferred_element_type=f32)
-    turns = jnp.mod(freq_across[None, :] * offsets[:, 0:1] + freq_down[None, :] * offsets[:, 1:2], BOX)
-    angle = turns.astype(f32) * (two_pi / BOX)
-    cos_base, sin_base = jnp.cos(angle), jnp.sin(angle)
-    real_part = particles[:, :pix].astype(f32)
-    imag_part = particles[:, pix:].astype(f32)
-    first = (real_part * cos_base + imag_part * sin_base) * ctf_rows
-    second = (imag_part * cos_base - real_part * sin_base) * ctf_rows
-    aligned = jnp.concatenate([first, second], axis=0).astype(bf16)
+    span = math.lcm(128, KY)
+    column = jnp.arange(span, dtype=jnp.int32)
+    across = jnp.concatenate([column // KY, jnp.full((128,), span // KY, jnp.int32)])
+    down = jnp.concatenate([column % KY - KY // 2, jnp.zeros((128,), jnp.int32)])
+    across, down = across.reshape(-1, 1, 128), down.reshape(-1, 1, 128)
+    phases = jnp.stack(rotation(offsets[None, :, 0:1], offsets[None, :, 1:2], across, down))
     own_refs = projections.reshape(classes, 2, pix).transpose(1, 0, 2).reshape(2 * classes, pix)
     listed = jnp.any(routes.T[:, None, :] == jnp.arange(n_orient, dtype=jnp.int32)[None, :, None], axis=0)
     chosen = jnp.arange(n_groups, dtype=jnp.int32)[:, None] == defocus_group[None, :]
@@ -471,10 +495,11 @@
     out, evidence = pl.pallas_call(
         lambda *r: fused_kernel(group, n_cls, own, pieces, *r),
         out_shape=(jax.ShapeDtypeStruct(piece, bf16), jax.ShapeDtypeStruct((8, 128), f32)),
-        in_specs=[spec] * 5,
+        in_specs=[spec] * 7,
         out_specs=(spec, spec),
         scratch_shapes=[
-            vmem((group,) + aligned.shape, bf16),
+            vmem((own, block), f32),
+            vmem((group, 2 * own, pix), bf16),
             vmem(stack, bf16),
             vmem((group,) + meta.shape, f32),
             vmem((kd, block), f32),
@@ -488,9 +513,9 @@
         ]
         + [dma((pieces, hops))] * 2 + [dma((pieces,))] * 2 + [dma((pieces, hops))] * 2 + [dma((group - 1,))] * 2
         + [dma((n_cls - 1,))] * 4 + [dma((2,))] + [dma((group - 1,))] * 2
-        + [dma((n_cls - 1,))] * 4 + [dma((2,)), dma((3,))],
+        + [dma((n_cls - 1,))] * 4 + [dma((2,)), dma((2,))],
         compiler_params=pltpu.CompilerParams(collective_id=0, has_side_effects=True, vmem_limit_bytes=VMEM_BYTES),
-    )(aligned, own_refs, meta, ctf, tables)
+    )(particles, phases, group_onehot, own_refs, meta, ctf, tables)
     log_evidence = evidence[0, :own]
     data_sum = out.reshape(2, classes, pix).transpose(1, 0, 2).reshape(classes, 1, 2 * pix)
     return (log_evidence, data_sum)

time: 61.5 us -> 61.5 us (level)
  matrix products: 6.05 us -> 0 us
  local copies, waits for them, and re-layouts: 3.01 us -> 6.37 us
  other arithmetic: 0.26 us -> 2.34 us
    dot_general x1 -> x0, matrix products: 6.05 us -> none  [per_device_halves(): ctf_rows = jnp.dot(group_onehot, ctf, preferred_element_type=f32)]
    unnamed x10 -> x6, local copies, waits for them, and re-layouts: 0.67 us -> 3.12 us
    reshape x1, local copies, waits for them, and re-layouts: 0.23 us -> 1.13 us  [per_device_halves(): projections.reshape(classes, 2, pix).transpose(1, 0, 2)]
    convert_element_type x0 -> x1, other arithmetic: none -> 0.73 us  [per_device_halves(): (defocus_group[:, None] == jnp.arange(n_groups, dtype=jnp.int32)[None, :]...]
    reduce_or x1, other arithmetic: 0.01 us -> 0.69 us  [per_device_halves(): jnp.any(routes.T[:, None, :] == jnp.arange(n_orient, dtype=jnp.int32)[Non...]
    eq x1, other arithmetic: 0.01 us -> 0.66 us  [per_device_halves(): jnp.arange(n_groups, dtype=jnp.int32)[:, None] == defocus_group[None, :]]
where the time goes in v3:
time: 61.5 us; the launch traced here: 61.2 us
  Pallas kernels  51.8 us (84%)
  local copies, waits for them, and re-layouts  6.37 us (10%)
  other arithmetic  2.34 us (4%)
  between operations  0.68 us (1%)
    pallas_call x1, Pallas kernels, per_device_halves(): pl.pallas_call(lambda *r: fused_kernel(group, n_cls, own, pieces, *r), ou...  51.8 us
    unnamed x6, local copies, waits for them, and re-layouts  3.12 us

profile of v3, /device:TPU:0, one launch (start us, length us, event | category | flops | bytes accessed | tf_op | source)
XLA Modules:
  0.0 61.2 jit_solution(688773267953512831)
XLA Ops:
  0.6 0.7 %fusion.5 = pred[8,12]{1,0:T(8,128)(4,1)S(1)} fusion(s32[4,12]{1,0:T(4,128)} %bitcast.19), kind=kLoop, calls=%fused_computation.10 | loop fusion | flops 672 | bytes 288 | tf_op jit(solution)/shard_map/reduce_or | solution.py:482
  1.3 0.7 %iota_compare_fusion.2 = pred[8,12]{1,0:T(8,128)(4,1)S(1)} fusion(s32[12]{0:T(128)} %param.10), kind=kLoop, calls=%fused_computation.15 | loop fusion | flops 96 | bytes 144 | tf_op jit(solution)/shard_map/eq | solution.py:483
  2.0 0.8 %slice_bitcast_fusion.2 = (s32[12]{0:T(128)S(1)}, s32[12]{0:T(128)S(1)}) fusion(s32[12,2]{0,1:T(2,128)} %param.11), kind=kLoop, calls=%fused_computation.32 | loop fusion | bytes 192 | tf_op jit(solution)/shard_map/mul | solution.py:29
  2.8 0.7 %fusion.6.r_2_ = bf16[12,8]{1,0:T(8,128)(2,1)S(1)} fusion(s32[12]{0:T(128)} %param.10), kind=kLoop, calls=%fused_computation.12 | loop fusion | flops 192 | bytes 240 | tf_op jit(solution)/shard_map/convert_element_type | solution.py:474
  3.5 0.2 fusion.4
  3.8 1.1 %reshape.80.r_3_ = bf16[4,16512]{1,0:T(4,128)(2,1)S(1)} reshape(bf16[2,2,16512]{2,1,0:T(2,128)(2,1)} %bitcast.17) | data formatting | bytes 264192 | tf_op jit(solution)/shard_map/reshape | solution.py:481
  4.9 0.0 copy-start
  4.9 1.2 %copy-done = bf16[12,33024]{1,0:T(8,128)(2,1)S(1)} copy-done((bf16[12,33024]{1,0:T(8,128)(2,1)S(1)}, bf16[12,33024]{1,0:T(8,128)(2,1)}, u32[]{:S(2)}) %copy-start) | copy-done | bytes 792600
  6.1 0.0 copy-start.1
  6.1 0.9 %copy-done.1 = bf16[8,16512]{1,0:T(8,128)(2,1)S(1)} copy-done((bf16[8,16512]{1,0:T(8,128)(2,1)S(1)}, bf16[8,16512]{1,0:T(8,128)(2,1)}, u32[]{:S(2)}) %copy-start.1) | copy-done | bytes 264216
  7.1 0.0 copy-start.2
  7.1 0.9 %copy-done.2 = f32[4,16512]{1,0:T(4,128)S(1)} copy-done((f32[4,16512]{1,0:T(4,128)S(1)}, f32[4,16512]{1,0:T(4,128)}, u32[]{:S(2)}) %copy-start.2) | copy-done | bytes 264216
  8.0 51.8 %shard_map.86 = (bf16[4,16512]{1,0:T(4,128)(2,1)S(1)}, f32[8,128]{1,0:T(8,128)S(1)}) custom-call(bf16[12,33024]{1,0:T(8,128)(2,1)S(1)} %copy-done, f32[2,4,12,128]{3,2,1,0:T(8,128)S(1)} %pad_maximum_fusion.r_1_, bf16[12,8]{1,0:T(8,128)(2,1)S(1)} %fusion.6.r_2_, bf16[4,16512]{1,0:T(4,128)(2,1)S(1)} %reshape.80.r_3_, f32[16,128]{1,0:T(8,128)S(1)} %pad_convert_fusion.r_4_, ...), custom_call_target="tpu_custom_call" | custom-call | tf_op jit(solution)/shard_map/pallas_call | solution.py:495
  59.8 0.5 slice_bitcast_fusion
  60.3 0.8 %reshape.81 = bf16[2,2,16512]{2,1,0:T(2,128)(2,1)} reshape(bf16[4,16512]{1,0:T(4,128)(2,1)S(1)} %get-tuple-element.5) | data formatting | bytes 264192 | tf_op jit(solution)/shard_map/reshape | solution.py:520
  (6 shorter events, 0.0 us)
Async XLA Ops:
  4.9 1.2 %copy-start = (bf16[12,33024]{1,0:T(8,128)(2,1)S(1)}, bf16[12,33024]{1,0:T(8,128)(2,1)}, u32[]{:S(2)}) copy-start(bf16[12,33024]{1,0:T(8,128)(2,1)} %r_0_.1) | copy-start | bytes 2377732
  6.1 1.0 %copy-start.1 = (bf16[8,16512]{1,0:T(8,128)(2,1)S(1)}, bf16[8,16512]{1,0:T(8,128)(2,1)}, u32[]{:S(2)}) copy-start(bf16[8,16512]{1,0:T(8,128)(2,1)} %r_5_.1) | copy-start | bytes 792580
  7.1 1.0 %copy-start.2 = (f32[4,16512]{1,0:T(4,128)S(1)}, f32[4,16512]{1,0:T(4,128)}, u32[]{:S(2)}) copy-start(f32[4,16512]{1,0:T(4,128)} %constant.49.clone.r_6_) | copy-start | bytes 792580
